TPU v7x, 32 devices: a whole 2x2x4 slice. The times are simulated.
32 devices in a mesh: group: 4 (over y, x), member: 8 (over z, core).
Axes of the slice: x: 2, y: 2, z: 4, core: 2. Of those that a mesh axis runs over, the one named last changes fastest.
Arguments:
- test_points: bfloat16 [32, 3, 1024], P(('group', 'member')), may hold values from 0 to 4
- test_basis: bfloat16 [32, 2, 1024, 256], P(('group', 'member')), may hold values from -0.25 to 0.25
- source_points: bfloat16 [32, 3, 1024], P(('group', 'member')), may hold values from 0 to 4
- source_basis: bfloat16 [32, 2, 1024, 256], P(('group', 'member')), may hold values from -0.1875 to 0.1875
- excitation: bfloat16 [32, 2, 256, 256], P(('group', 'member')), may hold values from -6 to 6
- preconditioner: bfloat16 [32, 256, 2, 256], P(('group', 'member')), may hold values from -0.25 to 0.25
- plan: int32 [2, 2], replicated, may hold values from 0 to 31, as said below
- solver_owner: int32 [32, 2, 4], P(('group', 'member')), may hold values from 0 to 7, as said below
Outputs:
- result: float32 [32, 256, 2, 256], P(('group', 'member'))
Inputs may be any that keep to these rules, and one draw needn't show every extreme that they name: `plan`: distinct domain indices. `solver_owner`: owners lie in the tile's own group. At most 2 of one device's 8 tiles go to one owner; in every group one owner takes exactly 2 tiles from every device of the group.
All inputs are finite; a program needn't handle non-finite values.
Results may differ from a plain program's by a relative error of at most 0.008.
Values may be sent and summed in bfloat16 or wider, within the bound.
No kernel may reach another device: no remote copies, remote signals or barrier semaphores. Data moves between devices by JAX's collectives and lax.ppermute only.
A program may use at most 128 MiB of HBM per device.

v0:
```python
import math

import jax
import jax.numpy as jnp
from jax import lax
from jax.sharding import PartitionSpec as P

CAP = 2


wave_number = 2.0 * math.pi
wire_radius = 0.05


def spread(value, axis, source):
    kept = jnp.where(lax.axis_index(axis) == source, value, 0).astype(value.dtype)
    return lax.psum(kept, axis)


def green_joined(points_test, points_source):
    near = points_test.astype(jnp.float32)
    far = points_source.astype(jnp.float32)
    dist_sq = jnp.zeros((near.shape[1], far.shape[1]), jnp.float32)
    for component in range(3):
        offset = near[component][:, None] - far[component][None, :]
        dist_sq = dist_sq + offset * offset
    distance = jnp.sqrt(dist_sq + wire_radius * wire_radius)
    weight = 1.0 / (4.0 * math.pi * distance)
    green_re = (jnp.cos(wave_number * distance) * weight).astype(jnp.bfloat16)
    green_im = (-jnp.sin(wave_number * distance) * weight).astype(jnp.bfloat16)
    return jnp.concatenate([green_re, green_im], axis=1)


def complex_block(real_part, imag_part):
    upper = jnp.concatenate([real_part, imag_part], axis=1)
    lower = jnp.concatenate([-imag_part, real_part], axis=1)
    return jnp.concatenate([upper, lower], axis=0)


def shards(
    test_points,
    test_basis,
    source_points,
    source_basis,
    excitation,
    preconditioner,
    plan,
    solver_owner,
):
    members = lax.axis_size("member")
    n_basis = source_basis.shape[3]
    n_excite = excitation.shape[3]
    own_points = test_points[0]
    own_basis = test_basis[0]
    domains_here = solver_owner.shape[1]
    per_domain = own_basis.shape[1] // domains_here
    owners = plan.reshape(-1)
    n_sources = owners.shape[0]
    bundle = (source_points[0], source_basis[0], excitation[0])
    left_basis = jnp.concatenate(
        [
            own_basis[0].reshape(domains_here, per_domain, n_basis),
            own_basis[1].reshape(domains_here, per_domain, n_basis),
        ],
        axis=1,
    )
    reduced_list = []
    coeff_list = []
    for source_slot in range(n_sources):
        owner_index = owners[source_slot]
        arrived = (
            spread(bundle[0], ("group", "member"), owner_index),
            spread(bundle[1], ("group", "member"), owner_index),
            spread(bundle[2], ("group", "member"), owner_index),
        )
        far_points, far_basis, far_coeff = arrived
        green = green_joined(own_points, far_points)
        basis_block = complex_block(far_basis[0], far_basis[1])
        half_field = jnp.dot(green, basis_block, preferred_element_type=jnp.float32).astype(
            jnp.bfloat16
        )
        half_split = half_field.reshape(domains_here, per_domain, 2 * n_basis)
        half_re = half_split[:, :, :n_basis]
        half_im = half_split[:, :, n_basis:]
        right_side = jnp.concatenate(
            [half_split, jnp.concatenate([half_im, -half_re], axis=2)], axis=1
        )
        reduced = jnp.einsum(
            "dpb,dpc->dbc", left_basis, right_side, preferred_element_type=jnp.float32
        ).astype(jnp.bfloat16)
        reduced_list.append(reduced)
        coeff_list.append(far_coeff)
    owner_ids = solver_owner[0].T.reshape(-1)
    tile_total = owner_ids.shape[0]
    all_tiles = jnp.concatenate(reduced_list, axis=0).reshape(tile_total, 2 * n_basis * n_basis)
    source_ids = jnp.arange(tile_total, dtype=jnp.int32) // domains_here
    same_owner = (owner_ids[:, None] == owner_ids[None, :]).astype(jnp.int32)
    lower_mask = (jnp.arange(tile_total)[None, :] < jnp.arange(tile_total)[:, None]).astype(
        jnp.int32
    )
    earlier = jnp.sum(same_owner * lower_mask, axis=1)
    slot_index = owner_ids * CAP + earlier
    placing = (slot_index[None, :] == jnp.arange(members * CAP, dtype=jnp.int32)[:, None]).astype(
        jnp.int32
    )
    packed = jnp.dot(
        placing.astype(jnp.bfloat16), all_tiles, preferred_element_type=jnp.float32
    ).astype(jnp.bfloat16)
    packed = packed.reshape(members, CAP, 2 * n_basis * n_basis)
    used = jnp.sum(placing, axis=1)
    labels = jnp.sum(placing * source_ids[None, :], axis=1) + (1 - used) * n_sources
    labels = labels.astype(jnp.float32).astype(jnp.bfloat16).reshape(members, CAP)
    got_tiles, got_labels = (
        lax.all_to_all(packed, "member", split_axis=0, concat_axis=0, tiled=True),
        lax.all_to_all(labels, "member", split_axis=0, concat_axis=0, tiled=True),
    )
    flat_tiles = got_tiles.reshape(members * CAP, 2 * n_basis * n_basis)
    flat_labels = got_labels.reshape(-1)
    wanted = jnp.arange(n_sources, dtype=jnp.float32).astype(jnp.bfloat16)
    picking = (flat_labels[None, :] == wanted[:, None]).astype(jnp.bfloat16)
    summed = jnp.dot(picking, flat_tiles, preferred_element_type=jnp.float32)
    summed = summed.reshape(n_sources, n_basis, 2 * n_basis)
    summed_high = summed.astype(jnp.bfloat16)
    summed_rest = (summed - summed_high.astype(jnp.float32)).astype(jnp.bfloat16)
    excite_all = jnp.stack([complex_block(coeff[0], coeff[1]) for coeff in coeff_list], axis=0)
    assembled = jnp.einsum(
        "sbk,ske->be", summed_high, excite_all, preferred_element_type=jnp.float32
    )
    assembled = assembled + jnp.einsum(
        "sbk,ske->be", summed_rest, excite_all, preferred_element_type=jnp.float32
    )
    assembled_low = assembled.astype(jnp.bfloat16)
    z_block = complex_block(assembled_low[:, :n_excite], assembled_low[:, n_excite:])
    inverse_rows = preconditioner[0].reshape(n_basis, 2 * n_basis)
    outcome = jnp.dot(inverse_rows, z_block, preferred_element_type=jnp.float32)
    return outcome.reshape(1, n_basis, 2, n_excite)


def solution(mesh):
    return jax.shard_map(
        shards,
        mesh=mesh,
        in_specs=(
            P(("group", "member"), None, None),
            P(("group", "member"), None, None, None),
            P(("group", "member"), None, None),
            P(("group", "member"), None, None, None),
            P(("group", "member"), None, None, None),
            P(("group", "member"), None, None, None),
            P(),
            P(("group", "member"), None, None),
        ),
        out_specs=P(("group", "member"), None, None, None),
        check_vma=False,
    )
```

profile of v0, /device:TPU:0, one launch (start us, length us, event | category | flops | bytes accessed | tf_op | source)
XLA Modules:
  0.0 319.2 jit_solution(7265426374540302880)
XLA Ops:
  6.5 0.8 copy.28
  7.3 0.1 reshape.152
  7.4 0.2 select_reduce_fusion.1
  7.6 0.1 convert_reduce_fusion
  7.7 0.7 convert_element_type.170
  8.4 6.3 %all-to-all-start = ((bf16[8,1,2]{2,1,0:T(2,128)(2,1)}), bf16[8,1,2]{2,1,0:T(2,128)(2,1)S(1)}, u32[]{:S(2)}, u32[]{:S(2)}) async-start(bf16[8,1,2]{2,1,0:T(2,128)(2,1)} %convert_element_type.170), calls=%async_computation | async-start | bytes 8192 | tf_op jit(solution)/shard_map/all_to_all | solution.py:115
  14.8 0.8 reshape.153
  15.5 0.6 fusion.147
  18.6 3.3 %select_bitcast_fusion.3 = (bf16[2,1024,256]{2,1,0:T(8,128)(2,1)}, bf16[2,1024,256]{2,1,0:T(8,128)(2,1)}, bf16[2,1024,256]{2,1,0:T(8,128)(2,1)}, bf16[2,1024,256]{2,1,0:T(8,128)(2,1)}) fusion(bf16[1,2,1024,256]{3,2,1,0:T(8,128)(2,1)} %param.11, pred[]{:T(512)S(6)} %eq.71, pred[]{:T(512)S(6)} %eq.72, pred[]{:T(512)S(6)} %eq.74, pred[]{:T(512)S(6)} %eq.73), kind=kLoop, calls=%fused_computation.109 | loop fusion | flops 2097152 | bytes 5242884 | tf_op jit(solution)/shard_map/jit(_where)/select_n | solution.py:16
  22.0 1.0 select_bitcast_fusion.7
  23.1 0.5 copy-done.4
  23.7 0.2 copy.31
  23.9 0.2 copy.30
  24.1 41.8 %all-reduce = (bf16[3,1024]{1,0:T(4,128)(2,1)S(1)}, bf16[3,1024]{1,0:T(4,128)(2,1)S(1)}, bf16[3,1024]{1,0:T(4,128)(2,1)S(1)}, bf16[3,1024]{1,0:T(4,128)(2,1)S(1)}) all-reduce(bf16[3,1024]{1,0:T(4,128)(2,1)S(1)} %get-tuple-element.88, ...), channel_id=1, replica_groups=mesh['group'=4,'member'=8] {'group','member'}, use_global_device_ids=true, to_apply=%region_3.4 | all-reduce | flops 12288 | bytes 49152 | tf_op jit(solution)/shard_map/psum | solution.py:17
  66.0 80.0 %multiply_convert_fusion.7 = (bf16[1024,1024]{1,0:T(8,128)(2,1)}, bf16[1024,1024]{1,0:T(8,128)(2,1)}, bf16[1024,1024]{1,0:T(8,128)(2,1)}, bf16[1024,1024]{1,0:T(...) fusion(f32[1024]{0:T(1024)S(1)} %bitcast.156, ...), kind=kLoop, calls=%fused_computation.33 | loop fusion | flops 71303168 | bytes 16838656 | tf_op jit(solution)/shard_map/convert_element_type | solution.py:29
  145.9 29.8 %all-reduce.4.cloned.1.call-done = (bf16[2,1024,256]{2,1,0:T(8,128)(2,1)}, bf16[2,1024,256]{2,1,0:T(8,128)(2,1)}, bf16[2,1024,256]{2,1,0:T(8,128)(2,1)}, bf16[2,...) async-done(((bf16[2,1024,256]{2,1,0:T(8,128)(2,1)}, ...) | async-done | bytes 5242896 | tf_op jit(solution)/shard_map/psum | solution.py:17
  175.8 1.8 slice_bitcast_fusion
  177.6 0.3 copy-done.3
  178.0 0.2 copy-done
  178.3 0.3 copy-done.1
  178.6 0.1 slice_bitcast_fusion.4
  178.7 0.1 fusion.133
  178.8 0.9 copy-done.19
  179.7 0.6 copy-done.20
  180.3 2.3 fusion.71
  182.7 0.1 fusion.141
  182.8 2.3 fusion.76
  185.2 2.3 fusion.81
  187.6 0.1 fusion.138
  187.7 2.3 fusion.86
  190.0 0.1 fusion.137
  190.1 0.7 fusion.91
  190.8 0.7 fusion.94
  191.5 0.7 fusion.97
  192.2 0.7 fusion.100
  192.9 0.3 maximum_bitcast_fusion
  193.2 1.2 copy.37
  194.4 3.1 convolution_convert_fusion
  197.4 5.5 %reshape.159 = bf16[8,2,131072]{2,1,0:T(2,128)(2,1)} reshape(bf16[16,131072]{1,0:T(8,128)(2,1)} %convolution_convert_fusion) | data formatting | bytes 8388608 | tf_op jit(solution)/shard_map/reshape | solution.py:109
  203.0 4.7 %all-to-all-start.1 = ((bf16[8,2,131072]{2,1,0:T(2,128)(2,1)}), bf16[8,2,131072]{2,1,0:T(2,128)(2,1)}, u32[]{:S(2)}, u32[]{:S(2)}) async-start(bf16[8,2,131072]{2,1,0:T(2,128)(2,1)} %reshape.159), calls=%async_computation.1 | async-start | bytes 8388608 | tf_op jit(solution)/shard_map/all_to_all | solution.py:114
  207.8 0.1 eq.67
  208.2 93.5 %all-to-all-done.1 = bf16[8,2,131072]{2,1,0:T(2,128)(2,1)} async-done(((bf16[8,2,131072]{2,1,0:T(2,128)(2,1)}), bf16[8,2,131072]{2,1,0:T(2,128)(2,1)}, u32[]{:S(2)}, u32[]{:S(2)}) %all-to-all-start.1) | async-done | bytes 4194336 | tf_op jit(solution)/shard_map/all_to_all | solution.py:114
  301.7 4.5 %reshape.160 = bf16[16,131072]{1,0:T(8,128)(2,1)} reshape(bf16[8,2,131072]{2,1,0:T(2,128)(2,1)} %all-to-all-done.1) | data formatting | bytes 8388608 | tf_op jit(solution)/shard_map/reshape | solution.py:117
  306.2 3.2 %subtract_convert_fusion = (bf16[4,256,512]{2,0,1:T(4,128)(2,1)S(1)}, bf16[4,256,512]{2,0,1:T(4,128)(2,1)S(1)}) fusion(bf16[2,256,8,512]{3,2,1,0:T(8,128)(2,1)} %bitcast.139, bf16[16]{0:T(256)(128)(2,1)S(1)} %eq.67, bf16[4]{0:T(256)(128)(2,1)S(1)} %iota_convert_fusion), kind=kOutput, calls=%fused_computation.90 | convolution fusion | flops 18874560 | bytes 6291496 | tf_op jit(solution)/shard_map/dot_general | solution.py:121
  309.4 0.8 convolution_bitcast_fusion
  310.2 0.8 fusion.104
  311.0 0.4 fusion.107
  311.4 1.0 copy.35
  (60 shorter events, 0.8 us)
Async XLA Ops:
  6.5 15.4 %copy-start.9 = (bf16[1,2,256,256]{3,2,1,0:T(8,128)(2,1)S(1)}, bf16[1,2,256,256]{3,2,1,0:T(8,128)(2,1)}, u32[]{:S(2)}) copy-start(bf16[1,2,256,256]{3,2,1,0:T(8,128)(2,1)} %param.12) | copy-start | bytes 786436
  8.4 194.6 %all-to-all-start = ((bf16[8,1,2]{2,1,0:T(2,128)(2,1)}), bf16[8,1,2]{2,1,0:T(2,128)(2,1)S(1)}, u32[]{:S(2)}, u32[]{:S(2)}) async-start(bf16[8,1,2]{2,1,0:T(2,128)(2,1)} %convert_element_type.170), calls=%async_computation | async-start | bytes 8192 | tf_op jit(solution)/shard_map/all_to_all | solution.py:115
  14.7 161.1 %all-reduce.4.cloned.1.call-start = ((), (), s32[]{:S(2)}) async-start(), calls=%async_computation.2 | async-start | bytes 10485760 | tf_op jit(solution)/shard_map/psum | solution.py:17
  22.0 1.0 copy-start.12
  22.0 1.1 copy-start.11
  22.0 1.6 copy-start.4
  175.8 1.9 copy-start.2
  175.8 2.2 copy-start.3
  175.8 2.5 copy-start
  175.8 2.8 copy-start.1
  178.0 1.7 copy-start.19
  178.0 2.4 copy-start.20
  180.3 2.4 copy-start.17
  180.3 2.4 copy-start.18
  182.8 2.4 copy-start.15
  182.8 2.4 copy-start.16
  185.2 2.4 copy-start.13
  185.2 2.4 copy-start.14
  203.0 4.7 %copy-start.10 = (bf16[1,256,2,256]{3,2,1,0:T(2,128)(2,1)S(1)}, bf16[1,256,2,256]{3,2,1,0:T(2,128)(2,1)}, u32[]{:S(2)}) copy-start(bf16[1,256,2,256]{3,2,1,0:T(2,128)(2,1)} %param.13) | copy-start | bytes 786436
  203.0 4.9 %copy-start.7 = (bf16[2,256,256]{2,1,0:T(8,128)(2,1)S(1)}, bf16[2,256,256]{2,1,0:T(8,128)(2,1)}, u32[]{:S(2)}) copy-start(bf16[2,256,256]{2,1,0:T(8,128)(2,1)} %get-tuple-element.15) | copy-start | bytes 786436
  203.0 4.9 %copy-start.8 = (bf16[2,256,256]{2,1,0:T(8,128)(2,1)S(1)}, bf16[2,256,256]{2,1,0:T(8,128)(2,1)}, u32[]{:S(2)}) copy-start(bf16[2,256,256]{2,1,0:T(8,128)(2,1)} %get-tuple-element.16) | copy-start | bytes 786436
  203.0 5.1 %copy-start.5 = (bf16[2,256,256]{2,1,0:T(8,128)(2,1)S(1)}, bf16[2,256,256]{2,1,0:T(8,128)(2,1)}, u32[]{:S(2)}) copy-start(bf16[2,256,256]{2,1,0:T(8,128)(2,1)} %get-tuple-element.17) | copy-start | bytes 786436
  203.0 5.1 %copy-start.6 = (bf16[2,256,256]{2,1,0:T(8,128)(2,1)S(1)}, bf16[2,256,256]{2,1,0:T(8,128)(2,1)}, u32[]{:S(2)}) copy-start(bf16[2,256,256]{2,1,0:T(8,128)(2,1)} %get-tuple-element.18) | copy-start | bytes 786436
  203.0 98.7 %all-to-all-start.1 = ((bf16[8,2,131072]{2,1,0:T(2,128)(2,1)}), bf16[8,2,131072]{2,1,0:T(2,128)(2,1)}, u32[]{:S(2)}, u32[]{:S(2)}) async-start(bf16[8,2,131072]{2,1,0:T(2,128)(2,1)} %reshape.159), calls=%async_computation.1 | async-start | bytes 8388608 | tf_op jit(solution)/shard_map/all_to_all | solution.py:114
Sparse Core Ops, SparseCore 0:
  23.1 152.6 all-reduce.3
where the time goes:
time: 320 us; the launch traced here: 319 us
  waiting for transfers between devices  123 us (38%)
  other arithmetic  85.5 us (27%)
  blocking collectives  41.8 us (13%)
  local copies, waits for them, and re-layouts  20.9 us (7%)
  matrix products  20.3 us (6%)
  between operations  16.4 us (5%)
  starting transfers between devices  11.1 us (3%)
    all_to_all x1, waiting for transfers between devices, shards(): lax.all_to_all(packed, 'member', split_axis=0, concat_axis=0, tiled=True)  93.5 us
    convert_element_type x1, other arithmetic, green_joined(): green_re = (jnp.cos(wave_number * distance) * weight).astype(jnp.bfloat16)  80 us
    psum x1, blocking collectives, spread(): return lax.psum(kept, axis)  41.8 us
    psum x1, waiting for transfers between devices, spread(): return lax.psum(kept, axis)  29.8 us
    dot_general x4, matrix products, shards(): jnp.dot(green, basis_block, preferred_element_type=jnp.float32)  9.3 us
  transfers between devices with their start and end apart: 3, of which 2 were waited for; matrix products, arithmetic and copies ran while one was open for 35% of the time, Pallas kernels for 0%

commit v1 on v0

v1 whole, which is shorter than its diff:
```python
import functools
import math

import jax
import jax.numpy as jnp
import numpy as np
from jax import lax
from jax.experimental import pallas as pl
from jax.experimental.pallas import tpu as pltpu
from jax.sharding import Mesh
from jax.sharding import PartitionSpec as P

CORES = 2
BLOCK = 256
PIECES = 2
FEATURES = 32
MIB = 2**20

wire_radius = 0.05
middle = 2.0
green_scale = 1.0 / (4.0 * math.pi)

COS_TERMS = (
    0.9999992215563883,
    -19.738982513245205,
    64.9287265171896,
    -85.27239586454552,
    58.794033467936565,
    -21.076773714433187,
)
SIN_TERMS = (
    6.283055796101308,
    -41.331214171938136,
    81.36681334731878,
    -74.47799414788796,
    32.78138228313484,
)

SHARE = 2 * CORES
COORDS = 3
CHIPS = ("group", "z")
EVERY = ("group", "z", "core")


def dot(left, right):
    return jnp.dot(left, right, preferred_element_type=jnp.float32)


def horner(value, terms):
    total = jnp.float32(terms[-1])
    for term in terms[-2::-1]:
        total = total * value + jnp.float32(term)
    return total


def green_pair(dist_sq):
    inverse = lax.rsqrt(dist_sq)
    distance = dist_sq * inverse
    turn = distance - jnp.round(distance)
    square = turn * turn
    real = horner(square, [green_scale * c for c in COS_TERMS]) * inverse
    imag = horner(square, [-green_scale * c for c in SIN_TERMS]) * (turn * inverse)
    return real.astype(jnp.bfloat16), imag.astype(jnp.bfloat16)


def split_terms(value, count):
    parts = []
    for _ in range(count):
        part = rounded(value)
        parts.append(part)
        value = value - part
    return parts


def point_terms(coords):
    high, low = split_terms(coords.astype(jnp.float32) - middle, 2)
    exact = high + low
    return high, low, jnp.sum(exact * exact, axis=0, keepdims=True)


def rounded(value):
    return value.astype(jnp.bfloat16).astype(jnp.float32)


def near_features(points):
    high, low, norm = point_terms(points)
    one = jnp.ones_like(norm)
    rows = split_terms(norm, 3) + [one, one, one]
    rows += [-2.0 * high, -2.0 * high, -2.0 * low, -2.0 * low]
    used = 6 + 4 * points.shape[0]
    rows.append(jnp.zeros((FEATURES - used, points.shape[1]), jnp.float32))
    return jnp.concatenate(rows, axis=0)


def far_features(points):
    high, low, norm = point_terms(points)
    norm = norm + jnp.float32(wire_radius * wire_radius)
    one = jnp.ones_like(norm)
    rows = [one, one, one] + split_terms(norm, 3)
    rows += [high, low, high, low]
    used = 6 + 4 * points.shape[0]
    rows.append(jnp.zeros((FEATURES - used, points.shape[1]), jnp.float32))
    return jnp.concatenate(rows, axis=0).astype(jnp.bfloat16)


def params(mib):
    return pltpu.CompilerParams(vmem_limit_bytes=mib * MIB)


TOKEN = jax.ShapeDtypeStruct((8, 128), jnp.float32)
SMALL = pl.CostEstimate(flops=1, bytes_accessed=1, transcendentals=0)


def whole(count):
    return [pl.BlockSpec(memory_space=pltpu.VMEM)] * count


def scalars(count):
    return [pl.BlockSpec(memory_space=pltpu.SMEM)] * count


def slot_place(slot, depths, info_ref, plan_ref):
    per_round = plan_ref.shape[1]
    owner = plan_ref[slot // per_round, slot % per_round]
    chip = owner // CORES
    return (chip // depths) ^ info_ref[1], (chip % depths) ^ info_ref[2], (owner % CORES) ^ info_ref[0]


def fold_kernel(core_ref, basis_ref, coeff_ref, keep_ref, send_ref):
    rows, cols = keep_ref.shape
    half = cols // 2
    right = jnp.concatenate([coeff_ref[0], coeff_ref[1]], axis=1)
    for turned, out_ref in ((1, send_ref), (0, keep_ref)):
        first = pl.multiple_of((core_ref[0] ^ turned) * rows, rows)
        upper = dot(basis_ref[0, pl.ds(first, rows)], right)
        lower = dot(basis_ref[1, pl.ds(first, rows)], right)
        out_ref[:, :half] = (upper[:, :half] - lower[:, half:]).astype(jnp.bfloat16)
        out_ref[:, half:] = (upper[:, half:] + lower[:, :half]).astype(jnp.bfloat16)


def fold(core, basis, coeff):
    points, n_basis = basis.shape[1:]
    n_excite = coeff.shape[2]
    shape = jax.ShapeDtypeStruct((points // CORES, 2 * n_excite), jnp.bfloat16)
    return pl.pallas_call(
        fold_kernel,
        in_specs=scalars(1) + whole(2),
        out_specs=whole(2),
        out_shape=[shape, shape],
        compiler_params=params(12),
        cost_estimate=SMALL,
    )(core, basis, coeff)


def pack(points):
    def kernel(*refs):
        *ins, out_ref = refs
        for place, in_ref in enumerate(ins):
            out_ref[place] = in_ref[...]

    return pl.pallas_call(
        kernel,
        out_shape=jax.ShapeDtypeStruct((len(points),) + points[0].shape, points[0].dtype),
        compiler_params=params(4),
        cost_estimate=SMALL,
    )(*points)


def spread(points, chips, depths):
    width = points.shape[1] // SHARE

    def kernel(points_ref, out_ref):
        for device in range(chips * CORES):
            place = (device % CORES) * 2 + (device // CORES) % depths % 2
            out_ref[device] = points_ref[:, place * width : (place + 1) * width]

    return pl.pallas_call(
        kernel,
        out_shape=jax.ShapeDtypeStruct((chips * CORES, points.shape[0], width), points.dtype),
        compiler_params=params(4),
        cost_estimate=SMALL,
    )(points)


def planned_features(plan, points):
    n_sources, width = plan.size, points.shape[2]

    def kernel(plan_ref, points_ref, out_ref):
        for slot in range(n_sources):
            owner = plan_ref[slot // plan.shape[1], slot % plan.shape[1]]
            out_ref[:, slot * width : (slot + 1) * width] = far_features(points_ref[owner])

    return pl.pallas_call(
        kernel,
        in_specs=scalars(1) + whole(1),
        out_specs=pl.BlockSpec(memory_space=pltpu.VMEM),
        out_shape=jax.ShapeDtypeStruct((FEATURES, n_sources * width), jnp.bfloat16),
        compiler_params=params(4),
        cost_estimate=SMALL,
    )(plan, points)


def primary_kernel(depths, info_ref, plan_ref, keep_ref, other_ref, *out_refs):
    core, group, depth = info_ref[0], info_ref[1], info_ref[2]
    first = (group * depths + depth) * CORES
    *out_refs, twin_ref = out_refs
    owners = [plan_ref[i, j] for i in range(plan_ref.shape[0]) for j in range(plan_ref.shape[1])]
    planned = jnp.int32(0)
    twin = jnp.int32(0)
    for place, owner in enumerate(owners):
        planned = planned | (owner == first).astype(jnp.int32)
        for other in owners[:place]:
            twin = twin | (owner // CORES == other // CORES).astype(jnp.int32)
    twin_ref[0] = twin
    own = planned ^ core
    for step, out_ref in enumerate(out_refs):
        for parity in range(2):
            span = slice(parity * (depths // 2), (parity + 1) * (depths // 2))

            @pl.when(own == 1)
            def _():
                out_ref[span] = keep_ref[parity, group ^ step]

            @pl.when(own == 0)
            def _():
                out_ref[span] = other_ref[parity, group ^ step]


def primary_parts(info, plan, depths, keep, other):
    _, count, _, per, cols = keep.shape
    shape = jax.ShapeDtypeStruct((depths, per, cols), keep.dtype)
    return pl.pallas_call(
        functools.partial(primary_kernel, depths),
        in_specs=scalars(2) + whole(2),
        out_specs=whole(count) + scalars(1),
        out_shape=[shape] * count + [jax.ShapeDtypeStruct((1,), jnp.int32)],
        compiler_params=params(6),
        cost_estimate=SMALL,
    )(info, plan, keep, other)


def regroup(info, parts, depths):
    n_groups = len(parts)
    shape = jax.ShapeDtypeStruct((n_groups,) + parts[0].shape[1:], parts[0].dtype)

    def kernel(info_ref, *refs):
        ins, outs, token_ref = refs[:n_groups], refs[n_groups:-1], refs[-1]
        token_ref[...] = jnp.zeros_like(token_ref)
        for step, out_ref in enumerate(outs):
            to = info_ref[2] ^ step
            for place, in_ref in enumerate(ins):
                out_ref[place] = in_ref[(to & 1) * (depths // 2) + (to >> 1)]

    return pl.pallas_call(
        kernel,
        in_specs=scalars(1) + whole(n_groups),
        out_specs=whole(depths + 1),
        out_shape=[shape] * depths + [TOKEN],
        compiler_params=params(6),
        cost_estimate=SMALL,
    )(info, *parts)


def pick(info, plan, second, arrived):
    n_sources, depths = plan.size, len(arrived)
    shape = jax.ShapeDtypeStruct((n_sources,) + arrived[0].shape[1:], arrived[0].dtype)

    def kernel(info_ref, plan_ref, second_ref, *refs):
        *ins, out_ref, sem = refs
        owners = [plan_ref[divmod(slot, plan.shape[1])] for slot in range(n_sources)]
        for slot in range(n_sources):
            across, along, _ = slot_place(slot, depths, info_ref, plan_ref)
            for step, in_ref in enumerate(ins):

                @pl.when(along == step)
                def _():
                    out_ref[slot] = in_ref[across]

            after = jnp.int32(0)
            for owner in owners:
                after = after | (owner == owners[slot] - 1).astype(jnp.int32)

            @pl.when((owners[slot] % CORES == 1) & (after == 1))
            def _():
                copy = pltpu.make_async_copy(
                    second_ref.at[owners[slot] // CORES], out_ref.at[slot], sem
                )
                copy.start()
                copy.wait()

    return pl.pallas_call(
        kernel,
        in_specs=scalars(2) + [pl.BlockSpec(memory_space=pl.ANY)] + whole(depths),
        out_specs=pl.BlockSpec(memory_space=pltpu.VMEM),
        out_shape=shape,
        scratch_shapes=[pltpu.SemaphoreType.DMA],
        compiler_params=params(6),
        cost_estimate=SMALL,
    )(info, plan, second, *arrived)


def prepare_kernel(place, points_ref, *refs):
    *basis_refs, near_ref, left_ref = refs
    n_domains = left_ref.shape[0]
    rows = basis_refs[0].shape[1] // n_domains
    n_basis = basis_refs[0].shape[2]
    near_ref[...] = near_features(points_ref[place, :COORDS]).T.astype(jnp.bfloat16)
    for domain in range(n_domains):
        span = slice(domain * rows, (domain + 1) * rows)
        real = basis_refs[0][0, span].T
        imag = basis_refs[-1][basis_refs[-1].shape[0] - 1, span].T
        left_ref[domain, :n_basis, :rows] = real
        left_ref[domain, :n_basis, rows:] = imag
        left_ref[domain, n_basis:, :rows] = -imag
        left_ref[domain, n_basis:, rows:] = real


def prepare(place, points, basis, n_domains):
    _, rows, n_basis = basis[0].shape
    return pl.pallas_call(
        functools.partial(prepare_kernel, place),
        out_shape=[
            jax.ShapeDtypeStruct((rows, FEATURES), jnp.bfloat16),
            jax.ShapeDtypeStruct((n_domains, 2 * n_basis, 2 * rows // n_domains), jnp.bfloat16),
        ],
        compiler_params=params(8),
        cost_estimate=SMALL,
    )(points, *basis)


def tested_kernel(n_devices, far_ref, *refs):
    nears, lefts, outs = (refs[i * n_devices : (i + 1) * n_devices] for i in range(3))
    token_ref, *green = refs[3 * n_devices :]
    token_ref[...] = jnp.zeros_like(token_ref)
    n_domains, size, _ = lefts[0].shape
    rows = nears[0].shape[0] // n_domains
    n_basis = size // 2
    blocks = far_ref.shape[1] // BLOCK
    work = [(i, d, b) for i in range(n_devices) for d in range(n_domains) for b in range(blocks)]

    def interact(index, piece):
        device, domain, block = work[index]
        part = rows // PIECES // 2
        span = slice(block * BLOCK, (block + 1) * BLOCK)
        into = green[index % 2]
        for first in range(2 * piece * part, 2 * (piece + 1) * part, part):
            near = nears[device][domain * rows + first : domain * rows + first + part]
            real, imag = green_pair(dot(near, far_ref[:, span]))
            into[first : first + part] = real
            into[rows + first : rows + first + part] = imag

    def test(index, piece):
        device, domain, block = work[index]
        start = (PIECES * block + piece) * BLOCK
        some = slice(piece * n_basis, (piece + 1) * n_basis)
        result = dot(lefts[device][domain, some], green[index % 2][...])
        outs[device][domain, :, start : start + BLOCK] = result.astype(jnp.bfloat16)

    for piece in range(PIECES):
        interact(0, piece)
    for index in range(len(work)):
        for piece in range(PIECES):
            test(index, piece)
            if index + 1 < len(work):
                interact(index + 1, piece)


def tested(far, nears, lefts):
    n_domains, size, twice = lefts[0].shape
    columns = far.shape[1]
    shape = jax.ShapeDtypeStruct((n_domains, size // 2, 2 * columns), jnp.bfloat16)
    return pl.pallas_call(
        functools.partial(tested_kernel, len(nears)),
        out_shape=[shape] * len(nears) + [TOKEN],
        scratch_shapes=[
            pltpu.VMEM((twice, BLOCK), jnp.bfloat16),
            pltpu.VMEM((twice, BLOCK), jnp.bfloat16),
        ],
        compiler_params=params(8),
        cost_estimate=pl.CostEstimate(
            flops=8 * len(nears) * n_domains * size * twice * columns,
            bytes_accessed=4 * MIB,
            transcendentals=0,
        ),
    )(far, *nears, *lefts)


def gather_kernel(n_tests, places, info_ref, *refs):
    owner_ref, tests = refs[0], refs[1 : n_tests + 1]
    *pieces, keep_ref, send_ref, far, total = refs[n_tests + 1 :]
    n_sources, twice, cols = far.shape
    width, half = twice // 2, cols // 2
    n_depth, n_basis, _ = keep_ref.shape
    n_domains = tests[0].shape[0]
    core, group, depth = info_ref[0], info_ref[1], info_ref[2]

    def fill(start, per, value):
        for slot in range(n_sources):
            block = value(slot)
            far[slot, pl.ds(start, per)] = block
            far[slot, pl.ds(width + start, per), :half] = -block[:, half:]
            far[slot, pl.ds(width + start, per), half:] = block[:, :half]

    if places is None:
        fill(0, width, lambda slot: pieces[0][slot])
    else:
        for piece, (across, steps) in zip(pieces, places):
            per = piece.shape[-2]
            for place, along in enumerate(steps):
                chip = (group ^ across) * (n_depth // 2) + ((depth ^ along) >> 1)
                start = pl.multiple_of(chip * per, per)
                fill(start, per, lambda slot: piece[place, slot])
    total[...] = jnp.zeros_like(total)

    def add_domain(domain, carry):
        for place, test in enumerate(tests):
            for slot in range(n_sources):
                left = test[domain, :, slot * twice : (slot + 1) * twice]
                owner = owner_ref[place, domain * n_sources + slot]
                total[owner] += dot(left, far[slot])
        return carry

    lax.fori_loop(0, n_domains, add_domain, 0)
    for step in range(n_depth):
        owner = CORES * (depth ^ step) + core
        keep_ref[step] = total[owner]
        send_ref[step] = total[owner ^ 1].astype(jnp.bfloat16)


def gather_products(info, owners, tests, pieces, places, depths, n_sources):
    n_domains, n_basis, columns = tests[0].shape
    cols = pieces[0].shape[-1]
    shape = (depths, n_basis, cols)
    return pl.pallas_call(
        functools.partial(gather_kernel, len(tests), places),
        in_specs=scalars(2) + whole(len(tests) + len(pieces)),
        out_specs=whole(2),
        out_shape=[
            jax.ShapeDtypeStruct(shape, jnp.float32),
            jax.ShapeDtypeStruct(shape, jnp.bfloat16),
        ],
        scratch_shapes=[
            pltpu.VMEM((n_sources, columns // n_sources, cols), jnp.bfloat16),
            pltpu.VMEM((CORES * depths, n_basis, cols), jnp.float32),
        ],
        compiler_params=params(14),
        cost_estimate=pl.CostEstimate(
            flops=2 * len(tests) * n_domains * n_basis * columns * cols,
            bytes_accessed=MIB,
            transcendentals=0,
        ),
    )(info, owners, *tests, *pieces)


def finish_kernel(inverse_ref, keep_ref, *refs):
    *others, out_ref = refs
    half = keep_ref.shape[2] // 2
    summed = keep_ref[0]
    for other in others:
        summed = summed + other[...].astype(jnp.float32)
    low = summed.astype(jnp.bfloat16)
    upper = dot(inverse_ref[:, : low.shape[0]], low)
    lower = dot(inverse_ref[:, low.shape[0] :], low)
    out_ref[:, 0] = upper[:, :half] - lower[:, half:]
    out_ref[:, 1] = upper[:, half:] + lower[:, :half]


def finish(inverse, keep, others):
    _, rows, cols = keep.shape
    return pl.pallas_call(
        finish_kernel,
        out_shape=jax.ShapeDtypeStruct((rows, 2, cols // 2), jnp.float32),
        compiler_params=params(12),
    )(inverse, keep, *others)


def partner(value, axis, step, size):
    return lax.ppermute(value, axis, [(i, i ^ step) for i in range(size)])


def shards(
    test_points,
    test_basis,
    source_points,
    source_basis,
    excitation,
    preconditioner,
    plan,
    solver_owner,
):
    groups, depths = lax.axis_size("group"), lax.axis_size("z")
    group, depth, core = lax.axis_index("group"), lax.axis_index("z"), lax.axis_index("core")
    chips = groups * depths
    n_domains, n_sources = solver_owner.shape[1:]
    src_points = source_points.shape[2]
    n_excite = excitation.shape[3]
    width = src_points // SHARE
    per = CORES * width // chips
    cols = 2 * n_excite
    info = jnp.stack([core, group, depth, depths]).astype(jnp.int32)
    def sibling(value):
        return partner(value, "core", 1, CORES)

    bases = [test_basis[0], sibling(test_basis[0]), partner(test_basis[0], "z", 1, depths)]

    keep, send = fold(info, source_basis[0], excitation[0])
    other = sibling(send)
    cut = (2, groups, depths // 2, per, cols)
    *parts, twin = primary_parts(info, plan, depths, keep.reshape(cut), other.reshape(cut))

    def rest_of_second(keep, other):
        first_planned = jnp.any(plan == (group * depths + depth) * CORES)
        rest = jnp.where(first_planned == (core == 0), other, keep).reshape(cut)
        rest = rest.transpose(1, 2, 0, 3, 4).reshape(chips, per, cols)
        return lax.all_to_all(rest, CHIPS, 0, 0, tiled=True)

    second = lax.cond(
        twin[0] > 0, rest_of_second, lambda _, other: other.reshape(chips, per, cols), keep, other
    )
    parts, source_points, test_points, solver_owner = lax.optimization_barrier(
        (parts, source_points, test_points, solver_owner)
    )
    parts = [parts[0]] + [partner(parts[k], "group", k, groups) for k in range(1, groups)]

    far_points = lax.all_to_all(spread(source_points[0], chips, depths), EVERY, 0, 0, tiled=True)
    n_tiles = n_domains * n_sources
    owner_row = solver_owner[0].reshape(1, n_tiles).astype(test_points.dtype)
    owner_row = jnp.pad(owner_row, ((0, 0), (0, src_points - n_tiles)))
    sides = jnp.concatenate([test_points[0], owner_row], axis=0)
    sides = pack((sides, sibling(sides)))

    parts, bases[2], sides = lax.optimization_barrier((parts, bases[2], sides))
    bases.append(sibling(bases[2]))
    *arrived, token = regroup(info, parts, depths)
    token, sides, far_points = lax.optimization_barrier((token, sides, far_points))
    packs = [sides, partner(sides, "z", 1, depths)]
    tile_owners = jnp.concatenate([side[:, COORDS, :n_tiles] for side in packs]).astype(jnp.int32)
    arrived = [arrived[0]] + [partner(arrived[k], "z", k, depths) for k in range(1, depths)]

    far = planned_features(plan, far_points)

    def test(place):
        near, left = prepare(
            place % CORES, packs[place // CORES], [bases[place]], n_domains
        )
        result, token = tested(far, [near], [left])
        tests.append(result)
        return token

    tests = []
    tokens = [test(0), test(1)]
    tokens, arrived = lax.optimization_barrier((tokens, arrived))
    mine = pick(info, plan, second, arrived)

    steps = list(range(0, depths, 2))
    held = jnp.stack([mine] + [partner(mine, "z", k, depths) for k in steps[1:]])
    token, held = lax.optimization_barrier((test(2), held))
    pieces = [held] + [partner(held, "group", k, groups) for k in range(1, groups)]
    places = [(k, steps) for k in range(groups)]
    test(3)
    if per % 16:
        half = depths // 2
        sorted_pieces = [[None] * half for _ in range(groups)]
        for piece, (across, steps) in zip(pieces, places):
            for place, along in enumerate(steps):
                sorted_pieces[across][along // 2] = piece[place]
        stacked = jnp.stack([jnp.stack(row) for row in sorted_pieces])
        stacked = stacked[group ^ jnp.arange(groups)][:, (depth // 2) ^ jnp.arange(half)]
        pieces = [stacked.transpose(2, 0, 1, 3, 4).reshape(n_sources, width, cols)]
        places = None
    inverse = preconditioner[0].reshape(-1, cols)

    keep, send = gather_products(info, tile_owners, tests, pieces, places, depths, n_sources)
    crossed = sibling(send)
    others = [crossed[0]]
    for step in reversed(range(1, depths)):
        low = (keep[step] + crossed[step].astype(jnp.float32)).astype(jnp.bfloat16)
        others.append(partner(low, "z", step, depths))
    return finish(inverse, keep, others)[None]


def solution(mesh):
    groups, members = mesh.devices.shape
    assert members % SHARE == 0
    fine = Mesh(mesh.devices.reshape(groups, members // CORES, CORES), ("group", "z", "core"))
    every = EVERY
    return jax.shard_map(
        shards,
        mesh=fine,
        in_specs=(
            P(every, None, None),
            P(every, None, None, None),
            P(every, None, None),
            P(every, None, None, None),
            P(every, None, None, None),
            P(every, None, None, None),
            P(),
            P(every, None, None),
        ),
        out_specs=P(every, None, None, None),
        check_vma=False,
    )
```

time: 320 us -> 111 us (0.35)
  waiting for transfers between devices: 123 us -> 37.9 us
  other arithmetic: 85.5 us -> 0.44 us
  blocking collectives: 41.8 us -> 0 us
  Pallas kernels: 0 us -> 38.9 us
  matrix products: 20.3 us -> 0 us
  starting transfers between devices: 11.1 us -> 27.4 us
  local copies, waits for them, and re-layouts: 20.9 us -> 5.12 us
  between operations: 16.4 us -> 0.88 us
    all_to_all x2 -> x1, waiting for transfers between devices: 93.5 us -> 4.71 us  [shards(): lax.all_to_all(spread(source_points[0], chips, depths), EVERY, 0, 0, tile...]
    convert_element_type x2 -> x3, other arithmetic: 80 us -> 0.33 us  [the longest x1 0.31 us: shards(): low = (keep[step] + crossed[step].astype(jnp.float32)).astype(jnp.bfloat16)]
    psum x1 -> x0, blocking collectives: 41.8 us -> none  [spread(): return lax.psum(kept, axis)]
    pallas_call x0 -> x17, Pallas kernels: none -> 38.9 us  [the longest x4 22.7 us: tested(): pl.pallas_call(functools.partial(tested_kernel, len(nears)), out_shape=[s...]
    ppermute x0 -> x20, waiting for transfers between devices: none -> 33.1 us  [partner(): return lax.ppermute(value, axis, [(i, i ^ step) for i in range(size)])]
    psum x1 -> x0, waiting for transfers between devices: 29.8 us -> none  [spread(): return lax.psum(kept, axis)]
    ppermute x0 -> x20, starting transfers between devices: none -> 22.5 us  [partner(): return lax.ppermute(value, axis, [(i, i ^ step) for i in range(size)])]
    dot_general x13 -> x0, matrix products: 20.3 us -> none  [the longest x4 9.3 us: shards(): jnp.dot(green, basis_block, preferred_element_type=jnp.float32)]
  transfers between devices with their start and end apart: 3 -> 21, of which waited for: 2 -> 9; matrix products, arithmetic and copies ran while one was open for 35% -> 0% of each run, Pallas kernels for 0% -> 28%
where the time goes in v1:
time: 111 us
  Pallas kernels  38.9 us (35%)
  waiting for transfers between devices  37.9 us (34%)
  starting transfers between devices  27.4 us (25%)
  local copies, waits for them, and re-layouts  5.12 us (5%)
    ppermute x20, waiting for transfers between devices, partner(): return lax.ppermute(value, axis, [(i, i ^ step) for i in range(size)])  33.1 us
    pallas_call x4, Pallas kernels, tested(): pl.pallas_call(functools.partial(tested_kernel, len(nears)), out_shape=[s...  22.7 us
    ppermute x20, starting transfers between devices, partner(): return lax.ppermute(value, axis, [(i, i ^ step) for i in range(size)])  22.5 us
    pallas_call x1, Pallas kernels, gather_products(): pl.pallas_call(functools.partial(gather_kernel, len(tests), places), in_s...  6.78 us
    unnamed x31, local copies, waits for them, and re-layouts  5.01 us
    all_to_all x1, starting transfers between devices, shards(): lax.all_to_all(spread(source_points[0], chips, depths), EVERY, 0, 0, tile...  4.84 us
    all_to_all x1, waiting for transfers between devices, shards(): lax.all_to_all(spread(source_points[0], chips, depths), EVERY, 0, 0, tile...  4.71 us
  transfers between devices with their start and end apart: 21, of which 9 were waited for; matrix products, arithmetic and copies ran while one was open for 0% of the time, Pallas kernels for 28%

profile of v1, /device:TPU:0, one launch (start us, length us, event | category | flops | bytes accessed | tf_op | source)
XLA Modules:
  0.0 110.6 jit_solution(16192866913905366485)
XLA Ops:
  0.0 3.1 %collective-permute-start.4 = (bf16[2,1024,256]{2,1,0:T(8,128)(2,1)}, bf16[2,1024,256]{2,1,0:T(8,128)(2,1)S(1)}, u32[]{:S(2)}, u32[]{:S(2)}) collective-permute-start(bf16[2,1024,256]{2,1,0:T(8,128)(2,1)} %bitcast.37), channel_id=1, source_target_pairs={{0,2},{2,0},{4,6},{6,4},{1,3},{3,1},{5,7},{7,5},{8,10},{10,8},{12,... | collective-permute-start | bytes 3145736 | tf_op jit(solution)/shard_map/ppermute | solution.py:478
  3.2 1.2 %copy-done = bf16[1,2,1024,256]{3,2,1,0:T(8,128)(2,1)S(1)} copy-done((bf16[1,2,1024,256]{3,2,1,0:T(8,128)(2,1)S(1)}, bf16[1,2,1024,256]{3,2,1,0:T(8,128)(2,1)}, u32[]{:S(2)}) %copy-start) | copy-done | bytes 1048600
  4.4 0.9 copy-done.2
  5.4 1.3 %shard_map.82 = (bf16[512,512]{1,0:T(8,128)(2,1)S(1)}, bf16[512,512]{1,0:T(8,128)(2,1)S(1)}) custom-call(s32[4]{0:T(128)S(1)} %pad_add_fusion.core_ref.info_ref, bf16[2,1024,256]{2,1,0:T(8,128)(2,1)S(1)} %bitcast.36, bf16[2,256,256]{2,1,0:T(8,128)(2,1)S(1)} %bitcast.42), custom_call_target="tpu_custom_call" | custom-call | flops 1 | bytes 1 | tf_op jit(solution)/shard_map/pallas_call | solution.py:145
  6.6 0.6 collective-permute-start
  7.2 1.5 %collective-permute-done = bf16[512,512]{1,0:T(8,128)(2,1)S(1)} collective-permute-done((bf16[512,512]{1,0:T(8,128)(2,1)S(1)}, bf16[512,512]{1,0:T(8,128)(2,1)S(1)}, u32[]{:S(2)}, u32[]{:S(2)}) %collective-permute-start) | collective-permute-done | bytes 524320 | tf_op jit(solution)/shard_map/ppermute | solution.py:478
  8.8 0.8 copy-done.7
  9.5 1.3 %shard_map.83 = (bf16[4,32,512]{2,1,0:T(8,128)(2,1)S(1)}, bf16[4,32,512]{2,1,0:T(8,128)(2,1)S(1)}, bf16[4,32,512]{2,1,0:T(8,128)(2,1)S(1)}, bf16[4,32,512]{2,1,0:T(8,128)(2,1)S(1)}, s32[1]{0:T(128)}) custom-call(s32[4]{0:T(128)S(1)} %pad_add_fusion.core_ref.info_ref, s32[2,2]{1,0:T(2,128)} %plan_ref.5, bf16[2,4,2,32,512]{4,3,2,1,0:T(8,128)(2,1)S(1)} %bitcast.46, ...), custom_call_target="tpu_custom_call" | custom-call | flops 1 | bytes 1 | tf_op jit(solution)/shard_map/pallas_call | solution.py:232
  10.9 0.6 copy-done.4
  11.6 0.7 copy-done.5
  12.2 0.6 copy-done.6
  13.0 0.4 collective-permute-start.5
  13.4 1.5 %collective-permute-start.1 = (bf16[4,32,512]{2,1,0:T(8,128)(2,1)}, bf16[4,32,512]{2,1,0:T(8,128)(2,1)S(1)}, u32[]{:S(2)}, u32[]{:S(2)}) collective-permute-start(bf16[4,32,512]{2,1,0:T(8,128)(2,1)} %copy-done.6), channel_id=1, source_target_pairs={{0,8},{8,0},{16,24},{24,16},{1,9},{9,1},{17,25},{25,17},{2,10},{10... | collective-permute-start | bytes 393224 | tf_op jit(solution)/shard_map/ppermute | solution.py:478
  14.9 1.5 %collective-permute-start.2 = (bf16[4,32,512]{2,1,0:T(8,128)(2,1)}, bf16[4,32,512]{2,1,0:T(8,128)(2,1)}, u32[]{:S(2)}, u32[]{:S(2)}) collective-permute-start(bf16[4,32,512]{2,1,0:T(8,128)(2,1)} %copy-done.5), channel_id=1, source_target_pairs={{0,16},{8,24},{16,0},{24,8},{1,17},{9,25},{17,1},{25,9},{2,18},{10... | collective-permute-start | bytes 393224 | tf_op jit(solution)/shard_map/ppermute | solution.py:478
  16.4 0.5 collective-permute-start.3
  16.9 0.6 shard_map.85
  18.2 4.8 %all-to-all-start.1 = ((bf16[32,3,256]{2,1,0:T(4,128)(2,1)}), bf16[32,3,256]{2,1,0:T(4,128)(2,1)S(1)}, u32[]{:S(2)}, u32[]{:S(2)}) async-start(bf16[32,3,256]{2,1,0:T(4,128)(2,1)} %shard_map.85), calls=%async_computation.1 | async-start | bytes 131072 | tf_op jit(solution)/shard_map/all_to_all | solution.py:525
  23.1 0.2 collective-permute-done.2.refs_2_
  23.3 3.4 %collective-permute-done.4.refs_0_ = bf16[2,1024,256]{2,1,0:T(8,128)(2,1)S(1)} collective-permute-done((bf16[2,1024,256]{2,1,0:T(8,128)(2,1)}, bf16[2,1024,256]{2,1,0:T(8,128)(2,1)S(1)}, u32[]{:S(2)}, u32[]{:S(2)}) %collective-permute-start.4) | collective-permute-done | bytes 1048608 | tf_op jit(solution)/shard_map/ppermute | solution.py:478
  26.7 4.7 %all-to-all-done.1.points_ref = bf16[32,3,256]{2,1,0:T(4,128)(2,1)S(1)} async-done(((bf16[32,3,256]{2,1,0:T(4,128)(2,1)}), bf16[32,3,256]{2,1,0:T(4,128)(2,1)S(1)}, u32[]{:S(2)}, u32[]{:S(2)}) %all-to-all-start.1) | async-done | bytes 49184 | tf_op jit(solution)/shard_map/all_to_all | solution.py:525
  31.4 0.5 collective-permute-start.6
  31.8 0.4 shard_map.87
  32.3 1.6 %shard_map.95 = (bf16[4,32,512]{2,1,0:T(8,128)(2,1)S(1)}, bf16[4,32,512]{2,1,0:T(8,128)(2,1)S(1)}, bf16[4,32,512]{2,1,0:T(8,128)(2,1)S(1)}, bf16[4,32,512]{2,1,0:T(8,128)(2,1)S(1)}, f32[8,128]{1,0:T(8,128)}) custom-call(s32[4]{0:T(128)S(1)} %pad_add_fusion.core_ref.info_ref, bf16[4,32,512]{2,1,0:T(8,128)(2,1)S(1)} %get-tuple-element.101.refs_0_, ...), custom_call_target="tpu_custom_call" | custom-call | flops 1 | bytes 1 | tf_op jit(solution)/shard_map/pallas_call | solution.py:254
  33.8 1.9 %collective-permute-start.10 = (bf16[4,32,512]{2,1,0:T(8,128)(2,1)S(1)}, bf16[4,32,512]{2,1,0:T(8,128)(2,1)S(1)}, u32[]{:S(2)}, u32[]{:S(2)}) collective-permute-start(bf16[4,32,512]{2,1,0:T(8,128)(2,1)S(1)} %get-tuple-element.107), channel_id=1, source_target_pairs={{0,4},{2,6},{4,0},{6,2},{1,5},{3,7},{5,1},{7,3},{8,12},{10,14},{12... | collective-permute-start | bytes 393224 | tf_op jit(solution)/shard_map/ppermute | solution.py:478
  35.7 2.1 %collective-permute-start.11 = (bf16[4,32,512]{2,1,0:T(8,128)(2,1)S(1)}, bf16[4,32,512]{2,1,0:T(8,128)(2,1)S(1)}, u32[]{:S(2)}, u32[]{:S(2)}) collective-permute-start(bf16[4,32,512]{2,1,0:T(8,128)(2,1)S(1)} %get-tuple-element.108), channel_id=1, source_target_pairs={{0,6},{2,4},{4,2},{6,0},{1,7},{3,5},{5,3},{7,1},{8,14},{10,12},{12... | collective-permute-start | bytes 393224 | tf_op jit(solution)/shard_map/ppermute | solution.py:478
  37.8 0.6 shard_map.86.far_ref
  38.5 0.5 shard_map.89
  38.9 5.7 %shard_map.90 = (bf16[2,256,2048]{2,1,0:T(8,128)(2,1)S(1)}, f32[8,128]{1,0:T(8,128)}) custom-call(bf16[32,1024]{1,0:T(8,128)(2,1)S(1)} %shard_map.86.far_ref, bf16[1024,32]{1,0:T(8,128)(2,1)S(1)} %get-tuple-element.90.refs_0_, bf16[2,512,1024]{2,1,0:T(8,128)(2,1)S(1)} %get-tuple-element.91.refs_1_), custom_call_target="tpu_custom_call" | custom-call | flops 8589934592 | bytes 4194304 | tf_op jit(solution)/shard_map/pallas_call | solution.py:372
  44.6 5.7 %shard_map.88 = (bf16[2,256,2048]{2,1,0:T(8,128)(2,1)S(1)}, f32[8,128]{1,0:T(8,128)}) custom-call(bf16[32,1024]{1,0:T(8,128)(2,1)S(1)} %shard_map.86.far_ref, bf16[1024,32]{1,0:T(8,128)(2,1)S(1)} %get-tuple-element.87.refs_0_, bf16[2,512,1024]{2,1,0:T(8,128)(2,1)S(1)} %get-tuple-element.88.refs_1_), custom_call_target="tpu_custom_call" | custom-call | flops 8589934592 | bytes 4194304 | tf_op jit(solution)/shard_map/pallas_call | solution.py:372
  50.3 0.4 shard_map.91
  50.8 0.9 shard_map.96
  51.7 2.4 %collective-permute-start.12 = (bf16[4,32,512]{2,1,0:T(8,128)(2,1)S(1)}, bf16[4,32,512]{2,1,0:T(8,128)(2,1)S(1)}, u32[]{:S(2)}, u32[]{:S(2)}) collective-permute-start(bf16[4,32,512]{2,1,0:T(8,128)(2,1)S(1)} %shard_map.96), channel_id=1, source_target_pairs={{0,4},{2,6},{4,0},{6,2},{1,5},{3,7},{5,1},{7,3},{8,12},{10,14},{12... | collective-permute-start | bytes 393224 | tf_op jit(solution)/shard_map/ppermute | solution.py:478
  54.1 5.7 %shard_map.92 = (bf16[2,256,2048]{2,1,0:T(8,128)(2,1)S(1)}, f32[8,128]{1,0:T(8,128)}) custom-call(bf16[32,1024]{1,0:T(8,128)(2,1)S(1)} %shard_map.86.far_ref, bf16[1024,32]{1,0:T(8,128)(2,1)S(1)} %get-tuple-element.94.refs_0_, bf16[2,512,1024]{2,1,0:T(8,128)(2,1)S(1)} %get-tuple-element.95.refs_1_), custom_call_target="tpu_custom_call" | custom-call | flops 8589934592 | bytes 4194304 | tf_op jit(solution)/shard_map/pallas_call | solution.py:372
  59.8 1.6 %collective-permute-done.12 = bf16[4,32,512]{2,1,0:T(8,128)(2,1)S(1)} collective-permute-done((bf16[4,32,512]{2,1,0:T(8,128)(2,1)S(1)}, bf16[4,32,512]{2,1,0:T(8,128)(2,1)S(1)}, u32[]{:S(2)}, u32[]{:S(2)}) %collective-permute-start.12) | collective-permute-done | bytes 131104 | tf_op jit(solution)/shard_map/ppermute | solution.py:478
  61.4 0.7 collective-permute-start.13
  62.2 0.7 collective-permute-start.14
  62.8 2.2 %collective-permute-start.15 = (bf16[2,4,32,512]{3,2,1,0:T(8,128)(2,1)S(1)}, bf16[2,4,32,512]{3,2,1,0:T(8,128)(2,1)S(1)}, u32[]{:S(2)}, u32[]{:S(2)}) collective-permute-start(bf16[2,4,32,512]{3,2,1,0:T(8,128)(2,1)S(1)} %pad_maximum_fusion.refs_5_), channel_id=1, source_target_pairs={{0,24},{8,16},{16,8},{24,0},{1,25},{9,17},{17,9},{25,1},{2,26},{10... | collective-permute-start | bytes 786440 | tf_op jit(solution)/shard_map/ppermute | solution.py:478
  65.0 0.5 shard_map.93
  65.5 5.7 %shard_map.94 = (bf16[2,256,2048]{2,1,0:T(8,128)(2,1)S(1)}, f32[8,128]{1,0:T(8,128)}) custom-call(bf16[32,1024]{1,0:T(8,128)(2,1)S(1)} %shard_map.86.far_ref, bf16[1024,32]{1,0:T(8,128)(2,1)S(1)} %get-tuple-element.97.refs_0_, bf16[2,512,1024]{2,1,0:T(8,128)(2,1)S(1)} %get-tuple-element.98.refs_1_), custom_call_target="tpu_custom_call" | custom-call | flops 8589934592 | bytes 4194304 | tf_op jit(solution)/shard_map/pallas_call | solution.py:372
  71.1 4.3 %collective-permute-done.14.refs_7_ = bf16[2,4,32,512]{3,2,1,0:T(8,128)(2,1)S(1)} collective-permute-done((bf16[2,4,32,512]{3,2,1,0:T(8,128)(2,1)S(1)}, bf16[2,4,32,512]{3,2,1,0:T(8,128)(2,1)S(1)}, u32[]{:S(2)}, u32[]{:S(2)}) %collective-permute-start.14) | collective-permute-done | bytes 262176 | tf_op jit(solution)/shard_map/ppermute | solution.py:478
  75.4 6.8 %shard_map.97 = (f32[4,256,512]{2,1,0:T(8,128)S(1)}, bf16[4,256,512]{2,1,0:T(8,128)(2,1)S(1)}) custom-call(s32[4]{0:T(128)S(1)} %pad_add_fusion.core_ref.info_ref, s32[4,8]{1,0:T(4,128)S(1)} %maximum_convert_fusion.refs_0_, bf16[2,256,2048]{2,1,0:T(8,128)(2,1)S(1)} %get-tuple-element.89.refs_1_, bf16[2,256,2048]{2,1,0:T(8,128)(2,1)S(1)} %get-tuple-element.92.refs_2_, ...), custom_call_target="tpu_custom_call" | custom-call | flops 4294967296 | bytes 1048576 | tf_op jit(solution)/shard_map/pallas_call | solution.py:434
  82.3 2.6 %collective-permute-done.16 = bf16[4,256,512]{2,1,0:T(8,128)(2,1)S(1)} collective-permute-done((bf16[4,256,512]{2,1,0:T(8,128)(2,1)S(1)}, bf16[4,256,512]{2,1,0:T(8,128)(2,1)S(1)}, u32[]{:S(2)}, u32[]{:S(2)}) %collective-permute-start.16) | collective-permute-done | bytes 1048608 | tf_op jit(solution)/shard_map/ppermute | solution.py:478
  85.0 0.3 fusion.2
  85.3 1.9 %collective-permute-start.17 = (bf16[256,512]{1,0:T(8,128)(2,1)S(1)}, bf16[256,512]{1,0:T(8,128)(2,1)S(1)}, u32[]{:S(2)}, u32[]{:S(2)}) collective-permute-start(bf16[256,512]{1,0:T(8,128)(2,1)S(1)} %get-tuple-element.117), channel_id=1, source_target_pairs={{0,6},{2,4},{4,2},{6,0},{1,7},{3,5},{5,3},{7,1},{8,14},{10,12},{12... | collective-permute-start | bytes 786440 | tf_op jit(solution)/shard_map/ppermute | solution.py:478
  87.2 2.6 %collective-permute-start.19 = (bf16[256,512]{1,0:T(8,128)(2,1)S(1)}, bf16[256,512]{1,0:T(8,128)(2,1)S(1)}, u32[]{:S(2)}, u32[]{:S(2)}) collective-permute-start(bf16[256,512]{1,0:T(8,128)(2,1)S(1)} %get-tuple-element.115), channel_id=1, source_target_pairs={{0,2},{2,0},{4,6},{6,4},{1,3},{3,1},{5,7},{7,5},{8,10},{10,8},{12,... | collective-permute-start | bytes 786440 | tf_op jit(solution)/shard_map/ppermute | solution.py:478
  89.8 6.6 %collective-permute-done.17.refs_1_ = bf16[256,512]{1,0:T(8,128)(2,1)S(1)} collective-permute-done((bf16[256,512]{1,0:T(8,128)(2,1)S(1)}, bf16[256,512]{1,0:T(8,128)(2,1)S(1)}, u32[]{:S(2)}, u32[]{:S(2)}) %collective-permute-start.17) | collective-permute-done | bytes 262176 | tf_op jit(solution)/shard_map/ppermute | solution.py:478
  96.4 12.8 %collective-permute-done.18.refs_2_ = bf16[256,512]{1,0:T(8,128)(2,1)S(1)} collective-permute-done((bf16[256,512]{1,0:T(8,128)(2,1)S(1)}, bf16[256,512]{1,0:T(8,128)(2,1)S(1)}, u32[]{:S(2)}, u32[]{:S(2)}) %collective-permute-start.18) | collective-permute-done | bytes 262176 | tf_op jit(solution)/shard_map/ppermute | solution.py:478
  109.3 1.3 %shard_map.98 = f32[256,2,256]{2,1,0:T(2,128)} custom-call(bf16[256,512]{1,0:T(8,128)(2,1)S(1)} %bitcast.40, f32[4,256,512]{2,1,0:T(8,128)S(1)} %get-tuple-element.113.keep_ref, bf16[256,512]{1,0:T(8,128)(2,1)S(1)} %slice_bitcast_fusion.refs_0_, bf16[256,512]{1,0:T(8,128)(2,1)S(1)} %collective-permute-done.17.refs_1_, ...), custom_call_target="tpu_custom_call" | custom-call | tf_op jit(solution)/shard_map/pallas_call | solution.py:470
  (53 shorter events, 0.5 us)
Async XLA Ops:
  0.0 18.2 %copy-start.11 = (s32[2,2]{1,0:T(2,128)S(1)}, s32[2,2]{1,0:T(2,128)}, u32[]{:S(2)}) copy-start(s32[2,2]{1,0:T(2,128)} %plan_ref.5) | copy-start | bytes 52
  0.0 13.0 %copy-start.12 = (bf16[1,3,1024]{2,1,0:T(4,128)(2,1)S(1)}, bf16[1,3,1024]{2,1,0:T(4,128)(2,1)}, u32[]{:S(2)}) copy-start(bf16[1,3,1024]{2,1,0:T(4,128)(2,1)} %param.10) | copy-start | bytes 18436
  0.0 16.9 %copy-start.3 = (bf16[1,3,1024]{2,1,0:T(4,128)(2,1)S(1)}, bf16[1,3,1024]{2,1,0:T(4,128)(2,1)}, u32[]{:S(2)}) copy-start(bf16[1,3,1024]{2,1,0:T(4,128)(2,1)} %param.12) | copy-start | bytes 18436
  0.0 12.9 %copy-start.13 = (s32[1,2,4]{2,1,0:T(2,128)S(1)}, s32[1,2,4]{2,1,0:T(2,128)}, u32[]{:S(2)}) copy-start(s32[1,2,4]{2,1,0:T(2,128)} %param.17) | copy-start | bytes 100
  0.0 26.6 %collective-permute-start.4 = (bf16[2,1024,256]{2,1,0:T(8,128)(2,1)}, bf16[2,1024,256]{2,1,0:T(8,128)(2,1)S(1)}, u32[]{:S(2)}, u32[]{:S(2)}) collective-permute-start(bf16[2,1024,256]{2,1,0:T(8,128)(2,1)} %bitcast.37), channel_id=1, source_target_pairs={{0,2},{2,0},{4,6},{6,4},{1,3},{3,1},{5,7},{7,5},{8,10},{10,8},{12,... | collective-permute-start | bytes 3145736 | tf_op jit(solution)/shard_map/ppermute | solution.py:478
  3.1 35.3 %collective-permute-start.7 = (bf16[2,1024,256]{2,1,0:T(8,128)(2,1)}, bf16[2,1024,256]{2,1,0:T(8,128)(2,1)S(1)}, u32[]{:S(2)}, u32[]{:S(2)}) collective-permute-start(bf16[2,1024,256]{2,1,0:T(8,128)(2,1)} %bitcast.38), channel_id=1, source_target_pairs={{0,1},{1,0},{2,3},{3,2},{4,5},{5,4},{6,7},{7,6},{8,9},{9,8},{10,11... | collective-permute-start | bytes 3145736 | tf_op jit(solution)/shard_map/ppermute | solution.py:478
  3.2 1.2 %copy-start = (bf16[1,2,1024,256]{3,2,1,0:T(8,128)(2,1)S(1)}, bf16[1,2,1024,256]{3,2,1,0:T(8,128)(2,1)}, u32[]{:S(2)}) copy-start(bf16[1,2,1024,256]{3,2,1,0:T(8,128)(2,1)} %param.13) | copy-start | bytes 3145732
  4.4 0.9 copy-start.2
  6.6 4.3 %copy-start.9 = (bf16[512,512]{1,0:T(8,128)(2,1)}, bf16[512,512]{1,0:T(8,128)(2,1)S(1)}, u32[]{:S(2)}) copy-start(bf16[512,512]{1,0:T(8,128)(2,1)S(1)} %get-tuple-element.123) | copy-start | bytes 1572868
  6.6 2.1 %collective-permute-start = (bf16[512,512]{1,0:T(8,128)(2,1)S(1)}, bf16[512,512]{1,0:T(8,128)(2,1)S(1)}, u32[]{:S(2)}, u32[]{:S(2)}) collective-permute-start(bf16[512,512]{1,0:T(8,128)(2,1)S(1)} %get-tuple-element.72), channel_id=1, source_target_pairs={{0,1},{1,0},{2,3},{3,2},{4,5},{5,4},{6,7},{7,6},{8,9},{9,8},{10,11... | collective-permute-start | bytes 1572872 | tf_op jit(solution)/shard_map/ppermute | solution.py:478
  8.7 0.8 copy-start.7
  10.9 0.7 copy-start.4
  11.6 0.7 copy-start.5
  12.2 0.6 copy-start.6
  12.9 19.0 %copy-start.1 = (bf16[1,2,1024,256]{3,2,1,0:T(8,128)(2,1)S(1)}, bf16[1,2,1024,256]{3,2,1,0:T(8,128)(2,1)}, u32[]{:S(2)}) copy-start(bf16[1,2,1024,256]{3,2,1,0:T(8,128)(2,1)} %param.11) | copy-start | bytes 3145732
  13.0 3.5 %collective-permute-start.5 = (bf16[4,1024]{1,0:T(4,128)(2,1)S(1)}, bf16[4,1024]{1,0:T(4,128)(2,1)S(1)}, u32[]{:S(2)}, u32[]{:S(2)}) collective-permute-start(bf16[4,1024]{1,0:T(4,128)(2,1)S(1)} %fusion.4.refs_0_), channel_id=1, source_target_pairs={{0,1},{1,0},{2,3},{3,2},{4,5},{5,4},{6,7},{7,6},{8,9},{9,8},{10,11... | collective-permute-start | bytes 24584 | tf_op jit(solution)/shard_map/ppermute | solution.py:478
  13.4 9.6 %collective-permute-start.1 = (bf16[4,32,512]{2,1,0:T(8,128)(2,1)}, bf16[4,32,512]{2,1,0:T(8,128)(2,1)S(1)}, u32[]{:S(2)}, u32[]{:S(2)}) collective-permute-start(bf16[4,32,512]{2,1,0:T(8,128)(2,1)} %copy-done.6), channel_id=1, source_target_pairs={{0,8},{8,0},{16,24},{24,16},{1,9},{9,1},{17,25},{25,17},{2,10},{10... | collective-permute-start | bytes 393224 | tf_op jit(solution)/shard_map/ppermute | solution.py:478
  14.9 8.4 %collective-permute-start.2 = (bf16[4,32,512]{2,1,0:T(8,128)(2,1)}, bf16[4,32,512]{2,1,0:T(8,128)(2,1)}, u32[]{:S(2)}, u32[]{:S(2)}) collective-permute-start(bf16[4,32,512]{2,1,0:T(8,128)(2,1)} %copy-done.5), channel_id=1, source_target_pairs={{0,16},{8,24},{16,0},{24,8},{1,17},{9,25},{17,1},{25,9},{2,18},{10... | collective-permute-start | bytes 393224 | tf_op jit(solution)/shard_map/ppermute | solution.py:478
  16.4 6.9 %collective-permute-start.3 = (bf16[4,32,512]{2,1,0:T(8,128)(2,1)}, bf16[4,32,512]{2,1,0:T(8,128)(2,1)}, u32[]{:S(2)}, u32[]{:S(2)}) collective-permute-start(bf16[4,32,512]{2,1,0:T(8,128)(2,1)} %copy-done.4), channel_id=1, source_target_pairs={{0,24},{8,16},{16,8},{24,0},{1,25},{9,17},{17,9},{25,1},{2,26},{10... | collective-permute-start | bytes 393224 | tf_op jit(solution)/shard_map/ppermute | solution.py:478
  18.2 13.2 %all-to-all-start.1 = ((bf16[32,3,256]{2,1,0:T(4,128)(2,1)}), bf16[32,3,256]{2,1,0:T(4,128)(2,1)S(1)}, u32[]{:S(2)}, u32[]{:S(2)}) async-start(bf16[32,3,256]{2,1,0:T(4,128)(2,1)} %shard_map.85), calls=%async_computation.1 | async-start | bytes 131072 | tf_op jit(solution)/shard_map/all_to_all | solution.py:525
  31.4 19.0 %collective-permute-start.6 = (bf16[2,4,1024]{2,1,0:T(4,128)(2,1)S(1)}, bf16[2,4,1024]{2,1,0:T(4,128)(2,1)S(1)}, u32[]{:S(2)}, u32[]{:S(2)}) collective-permute-start(bf16[2,4,1024]{2,1,0:T(4,128)(2,1)S(1)} %shard_map.84.points_ref), channel_id=1, source_target_pairs={{0,2},{2,0},{4,6},{6,4},{1,3},{3,1},{5,7},{7,5},{8,10},{10,8},{12,... | collective-permute-start | bytes 49160 | tf_op jit(solution)/shard_map/ppermute | solution.py:478
  33.8 16.9 %collective-permute-start.10 = (bf16[4,32,512]{2,1,0:T(8,128)(2,1)S(1)}, bf16[4,32,512]{2,1,0:T(8,128)(2,1)S(1)}, u32[]{:S(2)}, u32[]{:S(2)}) collective-permute-start(bf16[4,32,512]{2,1,0:T(8,128)(2,1)S(1)} %get-tuple-element.107), channel_id=1, source_target_pairs={{0,4},{2,6},{4,0},{6,2},{1,5},{3,7},{5,1},{7,3},{8,12},{10,14},{12... | collective-permute-start | bytes 393224 | tf_op jit(solution)/shard_map/ppermute | solution.py:478
  35.7 15.1 %collective-permute-start.11 = (bf16[4,32,512]{2,1,0:T(8,128)(2,1)S(1)}, bf16[4,32,512]{2,1,0:T(8,128)(2,1)S(1)}, u32[]{:S(2)}, u32[]{:S(2)}) collective-permute-start(bf16[4,32,512]{2,1,0:T(8,128)(2,1)S(1)} %get-tuple-element.108), channel_id=1, source_target_pairs={{0,6},{2,4},{4,2},{6,0},{1,7},{3,5},{5,3},{7,1},{8,14},{10,12},{12... | collective-permute-start | bytes 393224 | tf_op jit(solution)/shard_map/ppermute | solution.py:478
  37.8 13.0 %collective-permute-start.9 = (bf16[4,32,512]{2,1,0:T(8,128)(2,1)S(1)}, bf16[4,32,512]{2,1,0:T(8,128)(2,1)S(1)}, u32[]{:S(2)}, u32[]{:S(2)}) collective-permute-start(bf16[4,32,512]{2,1,0:T(8,128)(2,1)S(1)} %get-tuple-element.106), channel_id=1, source_target_pairs={{0,2},{2,0},{4,6},{6,4},{1,3},{3,1},{5,7},{7,5},{8,10},{10,8},{12,... | collective-permute-start | bytes 393224 | tf_op jit(solution)/shard_map/ppermute | solution.py:478
  38.4 26.6 %collective-permute-start.8 = (bf16[2,1024,256]{2,1,0:T(8,128)(2,1)S(1)}, bf16[2,1024,256]{2,1,0:T(8,128)(2,1)S(1)}, u32[]{:S(2)}, u32[]{:S(2)}) collective-permute-start(bf16[2,1024,256]{2,1,0:T(8,128)(2,1)S(1)} %collective-permute-done.4.refs_0_), channel_id=1, source_target_pairs={{0,1},{1,0},{2,3},{3,2},{4,5},{5,4},{6,7},{7,6},{8,9},{9,8},{10,11... | collective-permute-start | bytes 3145736 | tf_op jit(solution)/shard_map/ppermute | solution.py:478
  44.6 6.2 %copy-start.8 = (bf16[16,32,512]{2,1,0:T(8,128)(2,1)S(1)}, bf16[16,32,512]{2,1,0:T(8,128)(2,1)}, u32[]{:S(2)}) copy-start(bf16[16,32,512]{2,1,0:T(8,128)(2,1)} %get-tuple-element.124.second_ref) | copy-start | bytes 1572868
  51.7 9.7 %collective-permute-start.12 = (bf16[4,32,512]{2,1,0:T(8,128)(2,1)S(1)}, bf16[4,32,512]{2,1,0:T(8,128)(2,1)S(1)}, u32[]{:S(2)}, u32[]{:S(2)}) collective-permute-start(bf16[4,32,512]{2,1,0:T(8,128)(2,1)S(1)} %shard_map.96), channel_id=1, source_target_pairs={{0,4},{2,6},{4,0},{6,2},{1,5},{3,7},{5,1},{7,3},{8,12},{10,14},{12... | collective-permute-start | bytes 393224 | tf_op jit(solution)/shard_map/ppermute | solution.py:478
  61.4 9.7 %collective-permute-start.13 = (bf16[2,4,32,512]{3,2,1,0:T(8,128)(2,1)S(1)}, bf16[2,4,32,512]{3,2,1,0:T(8,128)(2,1)S(1)}, u32[]{:S(2)}, u32[]{:S(2)}) collective-permute-start(bf16[2,4,32,512]{3,2,1,0:T(8,128)(2,1)S(1)} %pad_maximum_fusion.refs_5_), channel_id=1, source_target_pairs={{0,8},{8,0},{16,24},{24,16},{1,9},{9,1},{17,25},{25,17},{2,10},{10... | collective-permute-start | bytes 786440 | tf_op jit(solution)/shard_map/ppermute | solution.py:478
  62.2 13.3 %collective-permute-start.14 = (bf16[2,4,32,512]{3,2,1,0:T(8,128)(2,1)S(1)}, bf16[2,4,32,512]{3,2,1,0:T(8,128)(2,1)S(1)}, u32[]{:S(2)}, u32[]{:S(2)}) collective-permute-start(bf16[2,4,32,512]{3,2,1,0:T(8,128)(2,1)S(1)} %pad_maximum_fusion.refs_5_), channel_id=1, source_target_pairs={{0,16},{8,24},{16,0},{24,8},{1,17},{9,25},{17,1},{25,9},{2,18},{10... | collective-permute-start | bytes 786440 | tf_op jit(solution)/shard_map/ppermute | solution.py:478
  62.8 12.6 %collective-permute-start.15 = (bf16[2,4,32,512]{3,2,1,0:T(8,128)(2,1)S(1)}, bf16[2,4,32,512]{3,2,1,0:T(8,128)(2,1)S(1)}, u32[]{:S(2)}, u32[]{:S(2)}) collective-permute-start(bf16[2,4,32,512]{3,2,1,0:T(8,128)(2,1)S(1)} %pad_maximum_fusion.refs_5_), channel_id=1, source_target_pairs={{0,24},{8,16},{16,8},{24,0},{1,25},{9,17},{17,9},{25,1},{2,26},{10... | collective-permute-start | bytes 786440 | tf_op jit(solution)/shard_map/ppermute | solution.py:478
  82.2 7.5 %copy-start.10 = (bf16[1,256,2,256]{3,2,1,0:T(2,128)(2,1)S(1)}, bf16[1,256,2,256]{3,2,1,0:T(2,128)(2,1)}, u32[]{:S(2)}) copy-start(bf16[1,256,2,256]{3,2,1,0:T(2,128)(2,1)} %param.15) | copy-start | bytes 786436
  82.2 2.7 %collective-permute-start.16 = (bf16[4,256,512]{2,1,0:T(8,128)(2,1)S(1)}, bf16[4,256,512]{2,1,0:T(8,128)(2,1)S(1)}, u32[]{:S(2)}, u32[]{:S(2)}) collective-permute-start(bf16[4,256,512]{2,1,0:T(8,128)(2,1)S(1)} %get-tuple-element.114), channel_id=1, source_target_pairs={{0,1},{1,0},{2,3},{3,2},{4,5},{5,4},{6,7},{7,6},{8,9},{9,8},{10,11... | collective-permute-start | bytes 3145736 | tf_op jit(solution)/shard_map/ppermute | solution.py:478
  85.3 11.2 %collective-permute-start.17 = (bf16[256,512]{1,0:T(8,128)(2,1)S(1)}, bf16[256,512]{1,0:T(8,128)(2,1)S(1)}, u32[]{:S(2)}, u32[]{:S(2)}) collective-permute-start(bf16[256,512]{1,0:T(8,128)(2,1)S(1)} %get-tuple-element.117), channel_id=1, source_target_pairs={{0,6},{2,4},{4,2},{6,0},{1,7},{3,5},{5,3},{7,1},{8,14},{10,12},{12... | collective-permute-start | bytes 786440 | tf_op jit(solution)/shard_map/ppermute | solution.py:478
  87.2 22.1 %collective-permute-start.18 = (bf16[256,512]{1,0:T(8,128)(2,1)S(1)}, bf16[256,512]{1,0:T(8,128)(2,1)S(1)}, u32[]{:S(2)}, u32[]{:S(2)}) collective-permute-start(bf16[256,512]{1,0:T(8,128)(2,1)S(1)} %get-tuple-element.116), channel_id=1, source_target_pairs={{0,4},{2,6},{4,0},{6,2},{1,5},{3,7},{5,1},{7,3},{8,12},{10,14},{12... | collective-permute-start | bytes 786440 | tf_op jit(solution)/shard_map/ppermute | solution.py:478
  87.2 22.1 %collective-permute-start.19 = (bf16[256,512]{1,0:T(8,128)(2,1)S(1)}, bf16[256,512]{1,0:T(8,128)(2,1)S(1)}, u32[]{:S(2)}, u32[]{:S(2)}) collective-permute-start(bf16[256,512]{1,0:T(8,128)(2,1)S(1)} %get-tuple-element.115), channel_id=1, source_target_pairs={{0,2},{2,0},{4,6},{6,4},{1,3},{3,1},{5,7},{7,5},{8,10},{10,8},{12,... | collective-permute-start | bytes 786440 | tf_op jit(solution)/shard_map/ppermute | solution.py:478

commit v2 on v1

--- a/solution.py
+++ b/solution.py
@@ -182,22 +182,22 @@
     )(points)
 
 
-def planned_features(plan, points):
+def planned_features(plan, points, after):
     n_sources, width = plan.size, points.shape[2]
 
-    def kernel(plan_ref, points_ref, out_ref):
+    def kernel(plan_ref, points_ref, after_ref, out_ref):
         for slot in range(n_sources):
             owner = plan_ref[slot // plan.shape[1], slot % plan.shape[1]]
             out_ref[:, slot * width : (slot + 1) * width] = far_features(points_ref[owner])
 
     return pl.pallas_call(
         kernel,
-        in_specs=scalars(1) + whole(1),
+        in_specs=scalars(1) + whole(2),
         out_specs=pl.BlockSpec(memory_space=pltpu.VMEM),
         out_shape=jax.ShapeDtypeStruct((FEATURES, n_sources * width), jnp.bfloat16),
         compiler_params=params(4),
         cost_estimate=SMALL,
-    )(plan, points)
+    )(plan, points, after)
 
 
 def primary_kernel(depths, info_ref, plan_ref, keep_ref, other_ref, *out_refs):
@@ -266,21 +266,22 @@
     shape = jax.ShapeDtypeStruct((n_sources,) + arrived[0].shape[1:], arrived[0].dtype)
 
     def kernel(info_ref, plan_ref, second_ref, *refs):
-        *ins, out_ref, sem = refs
+        *ins, out_ref, token_ref, sem = refs
+        token_ref[...] = jnp.zeros_like(token_ref)
         owners = [plan_ref[divmod(slot, plan.shape[1])] for slot in range(n_sources)]
         for slot in range(n_sources):
             across, along, _ = slot_place(slot, depths, info_ref, plan_ref)
+            before = jnp.int32(0)
+            for owner in owners:
+                before = before | (owner == owners[slot] - 1).astype(jnp.int32)
+            is_second = (owners[slot] % CORES) * before == 1
             for step, in_ref in enumerate(ins):
 
-                @pl.when(along == step)
+                @pl.when((along == step) & jnp.logical_not(is_second))
                 def _():
                     out_ref[slot] = in_ref[across]
 
-            after = jnp.int32(0)
-            for owner in owners:
-                after = after | (owner == owners[slot] - 1).astype(jnp.int32)
-
-            @pl.when((owners[slot] % CORES == 1) & (after == 1))
+            @pl.when(is_second)
             def _():
                 copy = pltpu.make_async_copy(
                     second_ref.at[owners[slot] // CORES], out_ref.at[slot], sem
@@ -291,12 +292,25 @@
     return pl.pallas_call(
         kernel,
         in_specs=scalars(2) + [pl.BlockSpec(memory_space=pl.ANY)] + whole(depths),
-        out_specs=pl.BlockSpec(memory_space=pltpu.VMEM),
-        out_shape=shape,
+        out_specs=whole(2),
+        out_shape=[shape, TOKEN],
         scratch_shapes=[pltpu.SemaphoreType.DMA],
         compiler_params=params(6),
         cost_estimate=SMALL,
     )(info, plan, second, *arrived)
+
+
+def hold(pieces):
+    def kernel(*refs):
+        *ins, out_ref, token_ref = refs
+        token_ref[...] = jnp.zeros_like(token_ref)
+        for place, in_ref in enumerate(ins):
+            out_ref[place] = in_ref[...]
+
+    shape = jax.ShapeDtypeStruct((len(pieces),) + pieces[0].shape, pieces[0].dtype)
+    return pl.pallas_call(
+        kernel, out_shape=[shape, TOKEN], compiler_params=params(6), cost_estimate=SMALL
+    )(*pieces)
 
 
 def prepare_kernel(place, points_ref, *refs):
@@ -328,7 +342,8 @@
     )(points, *basis)
 
 
-def tested_kernel(n_devices, far_ref, *refs):
+def tested_kernel(n_devices, n_after, far_ref, *refs):
+    refs = refs[n_after:]
     nears, lefts, outs = (refs[i * n_devices : (i + 1) * n_devices] for i in range(3))
     token_ref, *green = refs[3 * n_devices :]
     token_ref[...] = jnp.zeros_like(token_ref)
@@ -365,12 +380,12 @@
                 interact(index + 1, piece)
 
 
-def tested(far, nears, lefts):
+def tested(far, nears, lefts, after):
     n_domains, size, twice = lefts[0].shape
     columns = far.shape[1]
     shape = jax.ShapeDtypeStruct((n_domains, size // 2, 2 * columns), jnp.bfloat16)
     return pl.pallas_call(
-        functools.partial(tested_kernel, len(nears)),
+        functools.partial(tested_kernel, len(nears), len(after)),
         out_shape=[shape] * len(nears) + [TOKEN],
         scratch_shapes=[
             pltpu.VMEM((twice, BLOCK), jnp.bfloat16),
@@ -382,7 +397,7 @@
             bytes_accessed=4 * MIB,
             transcendentals=0,
         ),
-    )(far, *nears, *lefts)
+    )(far, *after, *nears, *lefts)
 
 
 def gather_kernel(n_tests, places, info_ref, *refs):
@@ -529,35 +544,35 @@
     sides = jnp.concatenate([test_points[0], owner_row], axis=0)
     sides = pack((sides, sibling(sides)))
 
-    parts, bases[2], sides = lax.optimization_barrier((parts, bases[2], sides))
-    bases.append(sibling(bases[2]))
+    parts, bases, sides = lax.optimization_barrier((parts, bases, sides))
     *arrived, token = regroup(info, parts, depths)
-    token, sides, far_points = lax.optimization_barrier((token, sides, far_points))
-    packs = [sides, partner(sides, "z", 1, depths)]
-    tile_owners = jnp.concatenate([side[:, COORDS, :n_tiles] for side in packs]).astype(jnp.int32)
+    token, far_points = lax.optimization_barrier((token, far_points))
+    packs = [sides]
     arrived = [arrived[0]] + [partner(arrived[k], "z", k, depths) for k in range(1, depths)]
 
-    far = planned_features(plan, far_points)
-
-    def test(place):
+    far = planned_features(plan, far_points, token)
+
+    def test(place, *after):
         near, left = prepare(
             place % CORES, packs[place // CORES], [bases[place]], n_domains
         )
-        result, token = tested(far, [near], [left])
+        result, _ = tested(far, [near], [left], after)
         tests.append(result)
-        return token
 
     tests = []
-    tokens = [test(0), test(1)]
-    tokens, arrived = lax.optimization_barrier((tokens, arrived))
-    mine = pick(info, plan, second, arrived)
+    test(0)
+    mine, token = pick(info, plan, second, arrived)
+    packs.append(partner(sides, "z", 1, depths))
+    bases.append(sibling(bases[2]))
+    tile_owners = jnp.concatenate([side[:, COORDS, :n_tiles] for side in packs]).astype(jnp.int32)
+    test(1, token)
 
     steps = list(range(0, depths, 2))
-    held = jnp.stack([mine] + [partner(mine, "z", k, depths) for k in steps[1:]])
-    token, held = lax.optimization_barrier((test(2), held))
+    held, token = hold([mine] + [partner(mine, "z", k, depths) for k in steps[1:]])
+    test(2, token)
+    test(3, token)
     pieces = [held] + [partner(held, "group", k, groups) for k in range(1, groups)]
     places = [(k, steps) for k in range(groups)]
-    test(3)
     if per % 16:
         half = depths // 2
         sorted_pieces = [[None] * half for _ in range(groups)]

time: 111 us -> 107 us (0.964)
  waiting for transfers between devices: 37.9 us -> 32.3 us
  Pallas kernels: 38.9 us -> 41.7 us
  local copies, waits for them, and re-layouts: 5.12 us -> 3.02 us
  starting transfers between devices: 27.4 us -> 28.6 us
    all_to_all x1, waiting for transfers between devices: 4.71 us -> 0.01 us  [shards(): lax.all_to_all(spread(source_points[0], chips, depths), EVERY, 0, 0, tile...]
    unnamed x31 -> x23, local copies, waits for them, and re-layouts: 5.01 us -> 2.91 us
    ppermute x20, starting transfers between devices: 22.5 us -> 23.8 us  [partner(): return lax.ppermute(value, axis, [(i, i ^ step) for i in range(size)])]
    pallas_call x4, Pallas kernels: 1.8 us -> 3.02 us  [prepare(): pl.pallas_call(functools.partial(prepare_kernel, place), out_shape=[jax.S...]
    pallas_call x5 -> x6, Pallas kernels: 23.3 us -> 23.5 us  [the longest x4 22.9 us: tested(): pl.pallas_call(functools.partial(tested_kernel, len(nears), len(after)),...]
  transfers between devices with their start and end apart: 21 -> 21, of which waited for: 9 -> 8; matrix products, arithmetic and copies ran while one was open for 0% -> 0% of each run, Pallas kernels for 28% -> 32%
where the time goes in v2:
time: 107 us
  Pallas kernels  41.7 us (39%)
  waiting for transfers between devices  32.3 us (30%)
  starting transfers between devices  28.6 us (27%)
  local copies, waits for them, and re-layouts  3.02 us (3%)
    ppermute x20, waiting for transfers between devices, partner(): return lax.ppermute(value, axis, [(i, i ^ step) for i in range(size)])  32.3 us
    ppermute x20, starting transfers between devices, partner(): return lax.ppermute(value, axis, [(i, i ^ step) for i in range(size)])  23.8 us
    pallas_call x4, Pallas kernels, tested(): pl.pallas_call(functools.partial(tested_kernel, len(nears), len(after)),...  22.9 us
    pallas_call x1, Pallas kernels, gather_products(): pl.pallas_call(functools.partial(gather_kernel, len(tests), places), in_s...  6.08 us
    all_to_all x1, starting transfers between devices, shards(): lax.all_to_all(spread(source_points[0], chips, depths), EVERY, 0, 0, tile...  4.84 us
    pallas_call x4, Pallas kernels, prepare(): pl.pallas_call(functools.partial(prepare_kernel, place), out_shape=[jax.S...  3.02 us
    unnamed x23, local copies, waits for them, and re-layouts  2.91 us
  transfers between devices with their start and end apart: 21, of which 8 were waited for; matrix products, arithmetic and copies ran while one was open for 0% of the time, Pallas kernels for 32%

profile of v2, /device:TPU:0, one launch (start us, length us, event | category | flops | bytes accessed | tf_op | source)
XLA Modules:
  0.0 107.0 jit_solution(16404625018274563229)
XLA Ops:
  0.0 0.5 collective-permute-start.4
  0.5 2.7 %collective-permute-start.5 = (bf16[2,1024,256]{2,1,0:T(8,128)(2,1)}, bf16[2,1024,256]{2,1,0:T(8,128)(2,1)S(1)}, u32[]{:S(2)}, u32[]{:S(2)}) collective-permute-start(bf16[2,1024,256]{2,1,0:T(8,128)(2,1)} %bitcast.36), channel_id=1, source_target_pairs={{0,2},{2,0},{4,6},{6,4},{1,3},{3,1},{5,7},{7,5},{8,10},{10,8},{12,... | collective-permute-start | bytes 3145736 | tf_op jit(solution)/shard_map/ppermute | solution.py:493
  3.2 0.1 pad_add_fusion.core_ref.info_ref
  3.3 1.2 %copy-done = bf16[1,2,1024,256]{3,2,1,0:T(8,128)(2,1)S(1)} copy-done((bf16[1,2,1024,256]{3,2,1,0:T(8,128)(2,1)S(1)}, bf16[1,2,1024,256]{3,2,1,0:T(8,128)(2,1)}, u32[]{:S(2)}) %copy-start) | copy-done | bytes 1048600
  4.5 0.9 copy-done.2
  5.4 2.0 %shard_map.82 = (bf16[512,512]{1,0:T(8,128)(2,1)}, bf16[512,512]{1,0:T(8,128)(2,1)S(1)}) custom-call(s32[4]{0:T(128)S(1)} %pad_add_fusion.core_ref.info_ref, bf16[2,1024,256]{2,1,0:T(8,128)(2,1)S(1)} %bitcast.34, bf16[2,256,256]{2,1,0:T(8,128)(2,1)S(1)} %bitcast.39), custom_call_target="tpu_custom_call" | custom-call | flops 1 | bytes 1 | tf_op jit(solution)/shard_map/pallas_call | solution.py:145
  7.5 0.2 collective-permute-start
  7.7 1.9 %collective-permute-done = bf16[512,512]{1,0:T(8,128)(2,1)} collective-permute-done((bf16[512,512]{1,0:T(8,128)(2,1)S(1)}, bf16[512,512]{1,0:T(8,128)(2,1)}, u32[]{:S(2)}, u32[]{:S(2)}) %collective-permute-start) | collective-permute-done | bytes 524320 | tf_op jit(solution)/shard_map/ppermute | solution.py:493
  9.5 2.1 %shard_map.83 = (bf16[4,32,512]{2,1,0:T(8,128)(2,1)S(1)}, bf16[4,32,512]{2,1,0:T(8,128)(2,1)}, bf16[4,32,512]{2,1,0:T(8,128)(2,1)}, bf16[4,32,512]{2,1,0:T(8,128)(2,1)}, s32[1]{0:T(128)}) custom-call(s32[4]{0:T(128)S(1)} %pad_add_fusion.core_ref.info_ref, s32[2,2]{1,0:T(2,128)} %plan_ref.5, bf16[2,4,2,32,512]{4,3,2,1,0:T(8,128)(2,1)} %bitcast.10.keep_ref, ...), custom_call_target="tpu_custom_call" | custom-call | flops 1 | bytes 1 | tf_op jit(solution)/shard_map/pallas_call | solution.py:232
  11.6 0.1 convert_element_type.56
  11.7 0.2 collective-permute-start.6
  12.0 1.5 %collective-permute-start.1 = (bf16[4,32,512]{2,1,0:T(8,128)(2,1)}, bf16[4,32,512]{2,1,0:T(8,128)(2,1)S(1)}, u32[]{:S(2)}, u32[]{:S(2)}) collective-permute-start(bf16[4,32,512]{2,1,0:T(8,128)(2,1)} %get-tuple-element.81), channel_id=1, source_target_pairs={{0,8},{8,0},{16,24},{24,16},{1,9},{9,1},{17,25},{25,17},{2,10},{10... | collective-permute-start | bytes 393224 | tf_op jit(solution)/shard_map/ppermute | solution.py:493
  13.5 1.5 %collective-permute-start.2 = (bf16[4,32,512]{2,1,0:T(8,128)(2,1)}, bf16[4,32,512]{2,1,0:T(8,128)(2,1)}, u32[]{:S(2)}, u32[]{:S(2)}) collective-permute-start(bf16[4,32,512]{2,1,0:T(8,128)(2,1)} %get-tuple-element.82), channel_id=1, source_target_pairs={{0,16},{8,24},{16,0},{24,8},{1,17},{9,25},{17,1},{25,9},{2,18},{10... | collective-permute-start | bytes 393224 | tf_op jit(solution)/shard_map/ppermute | solution.py:493
  15.0 0.5 collective-permute-start.3
  15.5 0.6 shard_map.86
  16.8 4.8 %all-to-all-start.1 = ((bf16[32,3,256]{2,1,0:T(4,128)(2,1)}), bf16[32,3,256]{2,1,0:T(4,128)(2,1)S(1)}, u32[]{:S(2)}, u32[]{:S(2)}) async-start(bf16[32,3,256]{2,1,0:T(4,128)(2,1)} %shard_map.86), calls=%async_computation.1 | async-start | bytes 131072 | tf_op jit(solution)/shard_map/all_to_all | solution.py:540
  21.6 0.4 collective-permute-done.2.refs_2_
  22.1 5.6 %collective-permute-done.5.refs_0_ = bf16[2,1024,256]{2,1,0:T(8,128)(2,1)S(1)} collective-permute-done((bf16[2,1024,256]{2,1,0:T(8,128)(2,1)}, bf16[2,1024,256]{2,1,0:T(8,128)(2,1)S(1)}, u32[]{:S(2)}, u32[]{:S(2)}) %collective-permute-start.5) | collective-permute-done | bytes 1048608 | tf_op jit(solution)/shard_map/ppermute | solution.py:493
  27.7 1.7 %shard_map.85 = (bf16[4,32,512]{2,1,0:T(8,128)(2,1)S(1)}, bf16[4,32,512]{2,1,0:T(8,128)(2,1)}, bf16[4,32,512]{2,1,0:T(8,128)(2,1)}, bf16[4,32,512]{2,1,0:T(8,128)(2,1)}, f32[8,128]{1,0:T(8,128)S(1)}) custom-call(s32[4]{0:T(128)S(1)} %pad_add_fusion.core_ref.info_ref, bf16[4,32,512]{2,1,0:T(8,128)(2,1)S(1)} %get-tuple-element.87.refs_0_, ...), custom_call_target="tpu_custom_call" | custom-call | flops 1 | bytes 1 | tf_op jit(solution)/shard_map/pallas_call | solution.py:254
  29.4 0.7 copy-done.3
  30.1 4.1 %collective-permute-start.10 = (bf16[4,32,512]{2,1,0:T(8,128)(2,1)}, bf16[4,32,512]{2,1,0:T(8,128)(2,1)S(1)}, u32[]{:S(2)}, u32[]{:S(2)}) collective-permute-start(bf16[4,32,512]{2,1,0:T(8,128)(2,1)} %get-tuple-element.103), channel_id=1, source_target_pairs={{0,6},{2,4},{4,2},{6,0},{1,7},{3,5},{5,3},{7,1},{8,14},{10,12},{12... | collective-permute-start | bytes 393224 | tf_op jit(solution)/shard_map/ppermute | solution.py:493
  34.2 0.6 collective-permute-start.9
  34.8 1.5 %collective-permute-start.7 = (bf16[2,4,1024]{2,1,0:T(4,128)(2,1)S(1)}, bf16[2,4,1024]{2,1,0:T(4,128)(2,1)S(1)}, u32[]{:S(2)}, u32[]{:S(2)}) collective-permute-start(bf16[2,4,1024]{2,1,0:T(4,128)(2,1)S(1)} %shard_map.84.points_ref), channel_id=1, source_target_pairs={{0,2},{2,0},{4,6},{6,4},{1,3},{3,1},{5,7},{7,5},{8,10},{10,8},{12,... | collective-permute-start | bytes 49160 | tf_op jit(solution)/shard_map/ppermute | solution.py:493
  36.3 0.4 shard_map.88
  36.7 0.6 shard_map.87.far_ref
  37.3 5.7 %shard_map.89 = (bf16[2,256,2048]{2,1,0:T(8,128)(2,1)S(1)}, f32[8,128]{1,0:T(8,128)}) custom-call(bf16[32,1024]{1,0:T(8,128)(2,1)S(1)} %shard_map.87.far_ref, bf16[1024,32]{1,0:T(8,128)(2,1)S(1)} %get-tuple-element.96.refs_0_, bf16[2,512,1024]{2,1,0:T(8,128)(2,1)S(1)} %get-tuple-element.97.refs_1_), custom_call_target="tpu_custom_call" | custom-call | flops 8589934592 | bytes 4194304 | tf_op jit(solution)/shard_map/pallas_call | solution.py:387
  43.0 0.4 shard_map.91
  43.5 0.5 shard_map.94
  44.0 0.5 collective-permute-done.9.refs_2_
  44.6 1.3 %shard_map.90 = (bf16[4,32,512]{2,1,0:T(8,128)(2,1)S(1)}, f32[8,128]{1,0:T(8,128)S(1)}) custom-call(s32[4]{0:T(128)S(1)} %pad_add_fusion.core_ref.info_ref, s32[2,2]{1,0:T(2,128)S(1)} %copy-done.7, bf16[16,32,512]{2,1,0:T(8,128)(2,1)} %get-tuple-element.130.second_ref, bf16[4,32,512]{2,1,0:T(8,128)(2,1)S(1)} %copy-done.4, ...), custom_call_target="tpu_custom_call" | custom-call | flops 1 | bytes 1 | tf_op jit(solution)/shard_map/pallas_call | solution.py:292
  45.9 2.5 %collective-permute-start.11 = (bf16[4,32,512]{2,1,0:T(8,128)(2,1)S(1)}, bf16[4,32,512]{2,1,0:T(8,128)(2,1)S(1)}, u32[]{:S(2)}, u32[]{:S(2)}) collective-permute-start(bf16[4,32,512]{2,1,0:T(8,128)(2,1)S(1)} %get-tuple-element.109.refs_0_), channel_id=1, source_target_pairs={{0,4},{2,6},{4,0},{6,2},{1,5},{3,7},{5,1},{7,3},{8,12},{10,14},{12... | collective-permute-start | bytes 393224 | tf_op jit(solution)/shard_map/ppermute | solution.py:493
  48.3 5.7 %shard_map.92 = (bf16[2,256,2048]{2,1,0:T(8,128)(2,1)S(1)}, f32[8,128]{1,0:T(8,128)}) custom-call(bf16[32,1024]{1,0:T(8,128)(2,1)S(1)} %shard_map.87.far_ref, f32[8,128]{1,0:T(8,128)S(1)} %get-tuple-element.104.refs_0_, bf16[1024,32]{1,0:T(8,128)(2,1)S(1)} %get-tuple-element.106.refs_1_, bf16[2,512,1024]{2,1,0:T(8,128)(2,1)S(1)} %get-tuple-element.107.refs_2_), custom_call_target="tpu_custom_call" | custom-call | flops 8589934592 | bytes 4194304 | tf_op jit(solution)/shard_map/pallas_call | solution.py:387
  54.0 0.7 collective-permute-done.11.refs_1_
  54.8 1.6 %collective-permute-start.13 = (bf16[2,4,32,512]{3,2,1,0:T(8,128)(2,1)S(1)}, bf16[2,4,32,512]{3,2,1,0:T(8,128)(2,1)S(1)}, u32[]{:S(2)}, u32[]{:S(2)}) collective-permute-start(bf16[2,4,32,512]{3,2,1,0:T(8,128)(2,1)S(1)} %get-tuple-element.118.refs_5_), channel_id=1, source_target_pairs={{0,8},{8,0},{16,24},{24,16},{1,9},{9,1},{17,25},{25,17},{2,10},{10... | collective-permute-start | bytes 786440 | tf_op jit(solution)/shard_map/ppermute | solution.py:493
  56.3 1.5 %collective-permute-start.14 = (bf16[2,4,32,512]{3,2,1,0:T(8,128)(2,1)S(1)}, bf16[2,4,32,512]{3,2,1,0:T(8,128)(2,1)S(1)}, u32[]{:S(2)}, u32[]{:S(2)}) collective-permute-start(bf16[2,4,32,512]{3,2,1,0:T(8,128)(2,1)S(1)} %get-tuple-element.118.refs_5_), channel_id=1, source_target_pairs={{0,16},{8,24},{16,0},{24,8},{1,17},{9,25},{17,1},{25,9},{2,18},{10... | collective-permute-start | bytes 786440 | tf_op jit(solution)/shard_map/ppermute | solution.py:493
  57.9 0.5 collective-permute-start.15
  58.3 5.7 %shard_map.95 = (bf16[2,256,2048]{2,1,0:T(8,128)(2,1)S(1)}, f32[8,128]{1,0:T(8,128)}) custom-call(bf16[32,1024]{1,0:T(8,128)(2,1)S(1)} %shard_map.87.far_ref, f32[8,128]{1,0:T(8,128)S(1)} %get-tuple-element.110.refs_0_, bf16[1024,32]{1,0:T(8,128)(2,1)S(1)} %get-tuple-element.112.refs_1_, bf16[2,512,1024]{2,1,0:T(8,128)(2,1)S(1)} %get-tuple-element.113.refs_2_), custom_call_target="tpu_custom_call" | custom-call | flops 8589934592 | bytes 4194304 | tf_op jit(solution)/shard_map/pallas_call | solution.py:387
  64.0 1.7 %shard_map.96 = (bf16[1024,32]{1,0:T(8,128)(2,1)S(1)}, bf16[2,512,1024]{2,1,0:T(8,128)(2,1)S(1)}) custom-call(bf16[2,4,1024]{2,1,0:T(4,128)(2,1)S(1)} %collective-permute-done.7.points_ref, bf16[2,1024,256]{2,1,0:T(8,128)(2,1)} %collective-permute-done.12.refs_0_), custom_call_target="tpu_custom_call" | custom-call | flops 1 | bytes 1 | tf_op jit(solution)/shard_map/pallas_call | solution.py:334
  65.7 5.9 %shard_map.97 = (bf16[2,256,2048]{2,1,0:T(8,128)(2,1)S(1)}, f32[8,128]{1,0:T(8,128)}) custom-call(bf16[32,1024]{1,0:T(8,128)(2,1)S(1)} %shard_map.87.far_ref, f32[8,128]{1,0:T(8,128)S(1)} %get-tuple-element.110.refs_0_, bf16[1024,32]{1,0:T(8,128)(2,1)S(1)} %get-tuple-element.115.refs_1_, bf16[2,512,1024]{2,1,0:T(8,128)(2,1)S(1)} %get-tuple-element.116.refs_2_), custom_call_target="tpu_custom_call" | custom-call | flops 8589934592 | bytes 4194304 | tf_op jit(solution)/shard_map/pallas_call | solution.py:387
  71.6 6.1 %shard_map.98 = (f32[4,256,512]{2,1,0:T(8,128)S(1)}, bf16[4,256,512]{2,1,0:T(8,128)(2,1)S(1)}) custom-call(s32[4]{0:T(128)S(1)} %pad_add_fusion.core_ref.info_ref, s32[4,8]{1,0:T(4,128)S(1)} %maximum_convert_fusion.refs_0_, bf16[2,256,2048]{2,1,0:T(8,128)(2,1)S(1)} %get-tuple-element.98.refs_1_, bf16[2,256,2048]{2,1,0:T(8,128)(2,1)S(1)} %get-tuple-element.108.refs_2_, ...), custom_call_target="tpu_custom_call" | custom-call | flops 4294967296 | bytes 1048576 | tf_op jit(solution)/shard_map/pallas_call | solution.py:449
  77.7 0.1 collective-permute-start.16
  77.8 2.6 %collective-permute-done.16 = bf16[4,256,512]{2,1,0:T(8,128)(2,1)S(1)} collective-permute-done((bf16[4,256,512]{2,1,0:T(8,128)(2,1)S(1)}, bf16[4,256,512]{2,1,0:T(8,128)(2,1)S(1)}, u32[]{:S(2)}, u32[]{:S(2)}) %collective-permute-start.16) | collective-permute-done | bytes 1048608 | tf_op jit(solution)/shard_map/ppermute | solution.py:493
  80.4 0.3 fusion.2
  80.7 2.7 %collective-permute-start.17 = (bf16[256,512]{1,0:T(8,128)(2,1)S(1)}, bf16[256,512]{1,0:T(8,128)(2,1)S(1)}, u32[]{:S(2)}, u32[]{:S(2)}) collective-permute-start(bf16[256,512]{1,0:T(8,128)(2,1)S(1)} %get-tuple-element.123), channel_id=1, source_target_pairs={{0,6},{2,4},{4,2},{6,0},{1,7},{3,5},{5,3},{7,1},{8,14},{10,12},{12... | collective-permute-start | bytes 786440 | tf_op jit(solution)/shard_map/ppermute | solution.py:493
  83.4 1.7 %collective-permute-start.19 = (bf16[256,512]{1,0:T(8,128)(2,1)S(1)}, bf16[256,512]{1,0:T(8,128)(2,1)S(1)}, u32[]{:S(2)}, u32[]{:S(2)}) collective-permute-start(bf16[256,512]{1,0:T(8,128)(2,1)S(1)} %get-tuple-element.121), channel_id=1, source_target_pairs={{0,2},{2,0},{4,6},{6,4},{1,3},{3,1},{5,7},{7,5},{8,10},{10,8},{12,... | collective-permute-start | bytes 786440 | tf_op jit(solution)/shard_map/ppermute | solution.py:493
  85.2 6.6 %collective-permute-done.17.refs_1_ = bf16[256,512]{1,0:T(8,128)(2,1)S(1)} collective-permute-done((bf16[256,512]{1,0:T(8,128)(2,1)S(1)}, bf16[256,512]{1,0:T(8,128)(2,1)S(1)}, u32[]{:S(2)}, u32[]{:S(2)}) %collective-permute-start.17) | collective-permute-done | bytes 262176 | tf_op jit(solution)/shard_map/ppermute | solution.py:493
  91.9 13.8 %collective-permute-done.18.refs_2_ = bf16[256,512]{1,0:T(8,128)(2,1)S(1)} collective-permute-done((bf16[256,512]{1,0:T(8,128)(2,1)S(1)}, bf16[256,512]{1,0:T(8,128)(2,1)S(1)}, u32[]{:S(2)}, u32[]{:S(2)}) %collective-permute-start.18) | collective-permute-done | bytes 262176 | tf_op jit(solution)/shard_map/ppermute | solution.py:493
  105.7 1.3 %shard_map.99 = f32[256,2,256]{2,1,0:T(2,128)} custom-call(bf16[256,512]{1,0:T(8,128)(2,1)S(1)} %bitcast.38, f32[4,256,512]{2,1,0:T(8,128)S(1)} %get-tuple-element.119.keep_ref, bf16[256,512]{1,0:T(8,128)(2,1)S(1)} %slice_bitcast_fusion.refs_0_, bf16[256,512]{1,0:T(8,128)(2,1)S(1)} %collective-permute-done.17.refs_1_, ...), custom_call_target="tpu_custom_call" | custom-call | tf_op jit(solution)/shard_map/pallas_call | solution.py:485
  (45 shorter events, 0.2 us)
Async XLA Ops:
  0.0 16.7 %copy-start.7 = (s32[2,2]{1,0:T(2,128)S(1)}, s32[2,2]{1,0:T(2,128)}, u32[]{:S(2)}) copy-start(s32[2,2]{1,0:T(2,128)} %plan_ref.5) | copy-start | bytes 52
  0.0 11.7 %copy-start.8 = (bf16[1,3,1024]{2,1,0:T(4,128)(2,1)S(1)}, bf16[1,3,1024]{2,1,0:T(4,128)(2,1)}, u32[]{:S(2)}) copy-start(bf16[1,3,1024]{2,1,0:T(4,128)(2,1)} %param.10) | copy-start | bytes 18436
  0.0 15.5 %copy-start.5 = (bf16[1,3,1024]{2,1,0:T(4,128)(2,1)S(1)}, bf16[1,3,1024]{2,1,0:T(4,128)(2,1)}, u32[]{:S(2)}) copy-start(bf16[1,3,1024]{2,1,0:T(4,128)(2,1)} %param.12) | copy-start | bytes 18436
  0.0 11.6 %copy-start.9 = (s32[1,2,4]{2,1,0:T(2,128)S(1)}, s32[1,2,4]{2,1,0:T(2,128)}, u32[]{:S(2)}) copy-start(s32[1,2,4]{2,1,0:T(2,128)} %param.17) | copy-start | bytes 100
  0.0 22.1 %collective-permute-start.4 = (bf16[2,1024,256]{2,1,0:T(8,128)(2,1)}, bf16[2,1024,256]{2,1,0:T(8,128)(2,1)S(1)}, u32[]{:S(2)}, u32[]{:S(2)}) collective-permute-start(bf16[2,1024,256]{2,1,0:T(8,128)(2,1)} %bitcast.35), channel_id=1, source_target_pairs={{0,1},{1,0},{2,3},{3,2},{4,5},{5,4},{6,7},{7,6},{8,9},{9,8},{10,11... | collective-permute-start | bytes 3145736 | tf_op jit(solution)/shard_map/ppermute | solution.py:493
  0.5 27.1 %collective-permute-start.5 = (bf16[2,1024,256]{2,1,0:T(8,128)(2,1)}, bf16[2,1024,256]{2,1,0:T(8,128)(2,1)S(1)}, u32[]{:S(2)}, u32[]{:S(2)}) collective-permute-start(bf16[2,1024,256]{2,1,0:T(8,128)(2,1)} %bitcast.36), channel_id=1, source_target_pairs={{0,2},{2,0},{4,6},{6,4},{1,3},{3,1},{5,7},{7,5},{8,10},{10,8},{12,... | collective-permute-start | bytes 3145736 | tf_op jit(solution)/shard_map/ppermute | solution.py:493
  3.3 1.2 %copy-start = (bf16[1,2,1024,256]{3,2,1,0:T(8,128)(2,1)S(1)}, bf16[1,2,1024,256]{3,2,1,0:T(8,128)(2,1)}, u32[]{:S(2)}) copy-start(bf16[1,2,1024,256]{3,2,1,0:T(8,128)(2,1)} %param.13) | copy-start | bytes 3145732
  4.5 0.9 copy-start.2
  7.5 2.0 %collective-permute-start = (bf16[512,512]{1,0:T(8,128)(2,1)S(1)}, bf16[512,512]{1,0:T(8,128)(2,1)}, u32[]{:S(2)}, u32[]{:S(2)}) collective-permute-start(bf16[512,512]{1,0:T(8,128)(2,1)S(1)} %get-tuple-element.75), channel_id=1, source_target_pairs={{0,1},{1,0},{2,3},{3,2},{4,5},{5,4},{6,7},{7,6},{8,9},{9,8},{10,11... | collective-permute-start | bytes 1572872 | tf_op jit(solution)/shard_map/ppermute | solution.py:493
  11.7 3.2 %collective-permute-start.6 = (bf16[4,1024]{1,0:T(4,128)(2,1)S(1)}, bf16[4,1024]{1,0:T(4,128)(2,1)S(1)}, u32[]{:S(2)}, u32[]{:S(2)}) collective-permute-start(bf16[4,1024]{1,0:T(4,128)(2,1)S(1)} %fusion.4.refs_0_), channel_id=1, source_target_pairs={{0,1},{1,0},{2,3},{3,2},{4,5},{5,4},{6,7},{7,6},{8,9},{9,8},{10,11... | collective-permute-start | bytes 24584 | tf_op jit(solution)/shard_map/ppermute | solution.py:493
  12.0 9.7 %collective-permute-start.1 = (bf16[4,32,512]{2,1,0:T(8,128)(2,1)}, bf16[4,32,512]{2,1,0:T(8,128)(2,1)S(1)}, u32[]{:S(2)}, u32[]{:S(2)}) collective-permute-start(bf16[4,32,512]{2,1,0:T(8,128)(2,1)} %get-tuple-element.81), channel_id=1, source_target_pairs={{0,8},{8,0},{16,24},{24,16},{1,9},{9,1},{17,25},{25,17},{2,10},{10... | collective-permute-start | bytes 393224 | tf_op jit(solution)/shard_map/ppermute | solution.py:493
  13.5 8.6 %collective-permute-start.2 = (bf16[4,32,512]{2,1,0:T(8,128)(2,1)}, bf16[4,32,512]{2,1,0:T(8,128)(2,1)}, u32[]{:S(2)}, u32[]{:S(2)}) collective-permute-start(bf16[4,32,512]{2,1,0:T(8,128)(2,1)} %get-tuple-element.82), channel_id=1, source_target_pairs={{0,16},{8,24},{16,0},{24,8},{1,17},{9,25},{17,1},{25,9},{2,18},{10... | collective-permute-start | bytes 393224 | tf_op jit(solution)/shard_map/ppermute | solution.py:493
  15.0 7.1 %collective-permute-start.3 = (bf16[4,32,512]{2,1,0:T(8,128)(2,1)}, bf16[4,32,512]{2,1,0:T(8,128)(2,1)}, u32[]{:S(2)}, u32[]{:S(2)}) collective-permute-start(bf16[4,32,512]{2,1,0:T(8,128)(2,1)} %get-tuple-element.83), channel_id=1, source_target_pairs={{0,24},{8,16},{16,8},{24,0},{1,25},{9,17},{17,9},{25,1},{2,26},{10... | collective-permute-start | bytes 393224 | tf_op jit(solution)/shard_map/ppermute | solution.py:493
  16.7 19.5 %copy-start.1 = (bf16[1,2,1024,256]{3,2,1,0:T(8,128)(2,1)S(1)}, bf16[1,2,1024,256]{3,2,1,0:T(8,128)(2,1)}, u32[]{:S(2)}) copy-start(bf16[1,2,1024,256]{3,2,1,0:T(8,128)(2,1)} %param.11) | copy-start | bytes 3145732
  16.8 19.5 %all-to-all-start.1 = ((bf16[32,3,256]{2,1,0:T(4,128)(2,1)}), bf16[32,3,256]{2,1,0:T(4,128)(2,1)S(1)}, u32[]{:S(2)}, u32[]{:S(2)}) async-start(bf16[32,3,256]{2,1,0:T(4,128)(2,1)} %shard_map.86), calls=%async_computation.1 | async-start | bytes 131072 | tf_op jit(solution)/shard_map/all_to_all | solution.py:540
  29.4 0.7 copy-start.3
  30.1 13.9 %collective-permute-start.10 = (bf16[4,32,512]{2,1,0:T(8,128)(2,1)}, bf16[4,32,512]{2,1,0:T(8,128)(2,1)S(1)}, u32[]{:S(2)}, u32[]{:S(2)}) collective-permute-start(bf16[4,32,512]{2,1,0:T(8,128)(2,1)} %get-tuple-element.103), channel_id=1, source_target_pairs={{0,6},{2,4},{4,2},{6,0},{1,7},{3,5},{5,3},{7,1},{8,14},{10,12},{12... | collective-permute-start | bytes 393224 | tf_op jit(solution)/shard_map/ppermute | solution.py:493
  34.2 9.8 %collective-permute-start.8 = (bf16[4,32,512]{2,1,0:T(8,128)(2,1)}, bf16[4,32,512]{2,1,0:T(8,128)(2,1)S(1)}, u32[]{:S(2)}, u32[]{:S(2)}) collective-permute-start(bf16[4,32,512]{2,1,0:T(8,128)(2,1)} %get-tuple-element.101), channel_id=1, source_target_pairs={{0,2},{2,0},{4,6},{6,4},{1,3},{3,1},{5,7},{7,5},{8,10},{10,8},{12,... | collective-permute-start | bytes 393224 | tf_op jit(solution)/shard_map/ppermute | solution.py:493
  34.2 10.3 %collective-permute-start.9 = (bf16[4,32,512]{2,1,0:T(8,128)(2,1)}, bf16[4,32,512]{2,1,0:T(8,128)(2,1)}, u32[]{:S(2)}, u32[]{:S(2)}) collective-permute-start(bf16[4,32,512]{2,1,0:T(8,128)(2,1)} %get-tuple-element.102), channel_id=1, source_target_pairs={{0,4},{2,6},{4,0},{6,2},{1,5},{3,7},{5,1},{7,3},{8,12},{10,14},{12... | collective-permute-start | bytes 393224 | tf_op jit(solution)/shard_map/ppermute | solution.py:493
  34.8 29.2 %collective-permute-start.12 = (bf16[2,1024,256]{2,1,0:T(8,128)(2,1)S(1)}, bf16[2,1024,256]{2,1,0:T(8,128)(2,1)}, u32[]{:S(2)}, u32[]{:S(2)}) collective-permute-start(bf16[2,1024,256]{2,1,0:T(8,128)(2,1)S(1)} %collective-permute-done.5.refs_0_), channel_id=1, source_target_pairs={{0,1},{1,0},{2,3},{3,2},{4,5},{5,4},{6,7},{7,6},{8,9},{9,8},{10,11... | collective-permute-start | bytes 3145736 | tf_op jit(solution)/shard_map/ppermute | solution.py:493
  34.8 8.7 %collective-permute-start.7 = (bf16[2,4,1024]{2,1,0:T(4,128)(2,1)S(1)}, bf16[2,4,1024]{2,1,0:T(4,128)(2,1)S(1)}, u32[]{:S(2)}, u32[]{:S(2)}) collective-permute-start(bf16[2,4,1024]{2,1,0:T(4,128)(2,1)S(1)} %shard_map.84.points_ref), channel_id=1, source_target_pairs={{0,2},{2,0},{4,6},{6,4},{1,3},{3,1},{5,7},{7,5},{8,10},{10,8},{12,... | collective-permute-start | bytes 49160 | tf_op jit(solution)/shard_map/ppermute | solution.py:493
  43.0 1.6 %copy-start.4 = (bf16[4,32,512]{2,1,0:T(8,128)(2,1)S(1)}, bf16[4,32,512]{2,1,0:T(8,128)(2,1)}, u32[]{:S(2)}) copy-start(bf16[4,32,512]{2,1,0:T(8,128)(2,1)} %copy-done.3) | copy-start | bytes 393220
  45.9 8.9 %collective-permute-start.11 = (bf16[4,32,512]{2,1,0:T(8,128)(2,1)S(1)}, bf16[4,32,512]{2,1,0:T(8,128)(2,1)S(1)}, u32[]{:S(2)}, u32[]{:S(2)}) collective-permute-start(bf16[4,32,512]{2,1,0:T(8,128)(2,1)S(1)} %get-tuple-element.109.refs_0_), channel_id=1, source_target_pairs={{0,4},{2,6},{4,0},{6,2},{1,5},{3,7},{5,1},{7,3},{8,12},{10,14},{12... | collective-permute-start | bytes 393224 | tf_op jit(solution)/shard_map/ppermute | solution.py:493
  54.8 16.8 %collective-permute-start.13 = (bf16[2,4,32,512]{3,2,1,0:T(8,128)(2,1)S(1)}, bf16[2,4,32,512]{3,2,1,0:T(8,128)(2,1)S(1)}, u32[]{:S(2)}, u32[]{:S(2)}) collective-permute-start(bf16[2,4,32,512]{3,2,1,0:T(8,128)(2,1)S(1)} %get-tuple-element.118.refs_5_), channel_id=1, source_target_pairs={{0,8},{8,0},{16,24},{24,16},{1,9},{9,1},{17,25},{25,17},{2,10},{10... | collective-permute-start | bytes 786440 | tf_op jit(solution)/shard_map/ppermute | solution.py:493
  56.3 15.2 %collective-permute-start.14 = (bf16[2,4,32,512]{3,2,1,0:T(8,128)(2,1)S(1)}, bf16[2,4,32,512]{3,2,1,0:T(8,128)(2,1)S(1)}, u32[]{:S(2)}, u32[]{:S(2)}) collective-permute-start(bf16[2,4,32,512]{3,2,1,0:T(8,128)(2,1)S(1)} %get-tuple-element.118.refs_5_), channel_id=1, source_target_pairs={{0,16},{8,24},{16,0},{24,8},{1,17},{9,25},{17,1},{25,9},{2,18},{10... | collective-permute-start | bytes 786440 | tf_op jit(solution)/shard_map/ppermute | solution.py:493
  57.9 13.7 %collective-permute-start.15 = (bf16[2,4,32,512]{3,2,1,0:T(8,128)(2,1)S(1)}, bf16[2,4,32,512]{3,2,1,0:T(8,128)(2,1)S(1)}, u32[]{:S(2)}, u32[]{:S(2)}) collective-permute-start(bf16[2,4,32,512]{3,2,1,0:T(8,128)(2,1)S(1)} %get-tuple-element.118.refs_5_), channel_id=1, source_target_pairs={{0,24},{8,16},{16,8},{24,0},{1,25},{9,17},{17,9},{25,1},{2,26},{10... | collective-permute-start | bytes 786440 | tf_op jit(solution)/shard_map/ppermute | solution.py:493
  77.7 7.5 %copy-start.6 = (bf16[1,256,2,256]{3,2,1,0:T(2,128)(2,1)S(1)}, bf16[1,256,2,256]{3,2,1,0:T(2,128)(2,1)}, u32[]{:S(2)}) copy-start(bf16[1,256,2,256]{3,2,1,0:T(2,128)(2,1)} %param.15) | copy-start | bytes 786436
  77.7 2.7 %collective-permute-start.16 = (bf16[4,256,512]{2,1,0:T(8,128)(2,1)S(1)}, bf16[4,256,512]{2,1,0:T(8,128)(2,1)S(1)}, u32[]{:S(2)}, u32[]{:S(2)}) collective-permute-start(bf16[4,256,512]{2,1,0:T(8,128)(2,1)S(1)} %get-tuple-element.120), channel_id=1, source_target_pairs={{0,1},{1,0},{2,3},{3,2},{4,5},{5,4},{6,7},{7,6},{8,9},{9,8},{10,11... | collective-permute-start | bytes 3145736 | tf_op jit(solution)/shard_map/ppermute | solution.py:493
  80.7 11.2 %collective-permute-start.17 = (bf16[256,512]{1,0:T(8,128)(2,1)S(1)}, bf16[256,512]{1,0:T(8,128)(2,1)S(1)}, u32[]{:S(2)}, u32[]{:S(2)}) collective-permute-start(bf16[256,512]{1,0:T(8,128)(2,1)S(1)} %get-tuple-element.123), channel_id=1, source_target_pairs={{0,6},{2,4},{4,2},{6,0},{1,7},{3,5},{5,3},{7,1},{8,14},{10,12},{12... | collective-permute-start | bytes 786440 | tf_op jit(solution)/shard_map/ppermute | solution.py:493
  83.4 22.2 %collective-permute-start.18 = (bf16[256,512]{1,0:T(8,128)(2,1)S(1)}, bf16[256,512]{1,0:T(8,128)(2,1)S(1)}, u32[]{:S(2)}, u32[]{:S(2)}) collective-permute-start(bf16[256,512]{1,0:T(8,128)(2,1)S(1)} %get-tuple-element.122), channel_id=1, source_target_pairs={{0,4},{2,6},{4,0},{6,2},{1,5},{3,7},{5,1},{7,3},{8,12},{10,14},{12... | collective-permute-start | bytes 786440 | tf_op jit(solution)/shard_map/ppermute | solution.py:493
  83.4 22.2 %collective-permute-start.19 = (bf16[256,512]{1,0:T(8,128)(2,1)S(1)}, bf16[256,512]{1,0:T(8,128)(2,1)S(1)}, u32[]{:S(2)}, u32[]{:S(2)}) collective-permute-start(bf16[256,512]{1,0:T(8,128)(2,1)S(1)} %get-tuple-element.121), channel_id=1, source_target_pairs={{0,2},{2,0},{4,6},{6,4},{1,3},{3,1},{5,7},{7,5},{8,10},{10,8},{12,... | collective-permute-start | bytes 786440 | tf_op jit(solution)/shard_map/ppermute | solution.py:493
